TPU v7x, 256 devices: a whole 4x4x8 slice. The times are simulated.
256 devices in a mesh: obs: 64 (over z, y, core), blk: 4 (over x).
Axes of the slice: x: 4, y: 4, z: 8, core: 2. Of those that a mesh axis runs over, the one named last changes fastest.
Arguments:
- jac_cols: float32 [2048, 262144], P('obs', 'blk'), may hold values from -6 to 6
- obs_group: int32 [4, 65536], P('blk', 'obs'), may hold values from 0 to 15
- group_weight: float32 [16], replicated, may hold values from 0.3 to 3
- pattern: int32 [4, 64, 16], P('blk', 'obs'), may hold values from 0 to 1, as said below
- pairs: int32 [128, 2], replicated, may hold values from 0 to 15, as said below
Outputs:
- normal: float32 [128, 128, 128], P('obs', 'blk')
Inputs may be any that keep to these rules, and one draw needn't show every extreme that they name: `pattern`: every panel marks between 2 and 16 blocks; in every draw some panel marks all 16. Distinct pairs, each with first entry <= second entry.
All inputs are finite; a program needn't handle non-finite values.
Results may differ from a plain program's by a relative error of at most 0.0003.
Values sent between devices are 32-bit elements; how exact they have to be, the bound alone decides.
No kernel may reach another device: no remote copies, remote signals or barrier semaphores. Data moves between devices by JAX's collectives and lax.ppermute only.
A program may use at most 128 MiB of HBM per device.

v0:
```python
import math

import jax
import jax.numpy as jnp
from jax import lax
from jax.sharding import PartitionSpec as P

BS = 128
NB = 16


def make_tiles(jblocks, wblocks, marks, scale):

    def group_tiles(pair_rows):
        first = pair_rows[:, 0]
        second = pair_rows[:, 1]
        prod = jnp.einsum(
            "pao,pbo->pab",
            jblocks[first],
            wblocks[second],
            precision=lax.Precision.HIGHEST,
            preferred_element_type=jnp.float32,
        )
        factor = marks[first] * marks[second] * scale
        return prod * factor[:, None, None]

    def run(pair_rows):
        count = pair_rows.shape[0]
        width = math.gcd(count, 16)
        steps = count // width
        grouped = pair_rows.reshape(steps, width, 2)
        result = lax.map(group_tiles, grouped)
        return result.reshape((count,) + result.shape[2:])

    return run


def on_device(jac_cols, obs_group, group_weight, pattern, pairs):
    jac = lax.all_to_all(jac_cols, "obs", split_axis=1, concat_axis=0, tiled=True)
    obs_dev = jac.shape[1]
    total_obs = obs_dev * lax.axis_size("obs") * lax.axis_size("blk")
    scale = 1.0 / math.sqrt(total_obs)
    squared = group_weight * group_weight
    onehot = (
        obs_group[0][:, None] == jnp.arange(group_weight.shape[0], dtype=jnp.int32)[None, :]
    ).astype(jnp.float32)
    weights = jnp.sum(onehot * squared[None, :], axis=1)
    jblocks = jac.reshape(NB, BS, obs_dev)
    wblocks = (jac * weights[None, :]).reshape(NB, BS, obs_dev)
    marks = pattern[0, 0].astype(jnp.float32)
    run = make_tiles(jblocks, wblocks, marks, scale)
    owned = lax.psum_scatter(run(pairs), "obs", scatter_dimension=0, tiled=True)
    return lax.psum_scatter(owned, "blk", scatter_dimension=1, tiled=True)


def solution(mesh):
    return jax.shard_map(
        on_device,
        mesh=mesh,
        in_specs=(P("obs", "blk"), P("blk", "obs"), P(), P("blk", "obs", None), P()),
        out_specs=P("obs", "blk", None),
        check_vma=False,
    )
```

profile of v0, /device:TPU:6, one launch (start us, length us, event | category | flops | bytes accessed | tf_op | source)
XLA Modules:
  0.0 633.2 jit_solution(5510969876927868154)
XLA Ops:
  6.5 8.3 %copy.14 = f32[4,64,8,1024]{3,2,0,1:T(8,128)} copy(f32[4,64,8,1024]{3,2,1,0:T(8,128)} %bitcast.37) | data formatting | bytes 16777216 | tf_op jit(solution)/shard_map/all_to_all | solution.py:39
  14.8 12.5 %all-to-all-start = ((f32[32,64,1024]{2,0,1:T(8,128)}), f32[32,64,1024]{2,0,1:T(8,128)}, u32[]{:S(2)}, u32[]{:S(2)}) async-start(f32[32,64,1024]{2,0,1:T(8,128)} %bitcast.36), calls=%async_computation | async-start | bytes 16777216 | tf_op jit(solution)/shard_map/all_to_all | solution.py:39
  27.6 185.8 %all-to-all-done = f32[32,64,1024]{2,0,1:T(8,128)} async-done(((f32[32,64,1024]{2,0,1:T(8,128)}), f32[32,64,1024]{2,0,1:T(8,128)}, u32[]{:S(2)}, u32[]{:S(2)}) %all-to-all-start) | async-done | bytes 8388640 | tf_op jit(solution)/shard_map/all_to_all | solution.py:39
  213.4 8.5 %broadcast_multiply_fusion = f32[16,128,1024]{2,1,0:T(8,128)} fusion(f32[16,128,1024]{2,1,0:T(8,128)} %bitcast.5, f32[1024]{0:T(1024)S(1)} %select_reduce_fusion), kind=kLoop, calls=%fused_computation.16 | loop fusion | flops 2097152 | bytes 16781312 | tf_op jit(solution)/shard_map/mul | solution.py:49
  221.9 233.5 %while.10 = (s32[]{:T(128)}, f32[8,16,128,128]{3,2,1,0:T(8,128)}, s32[8,16,2]{1,0,2:T(8,128)S(1)}, f32[16,128,1024]{2,1,0:T(8,128)}, f32[16,128,1024]{2,1,0:T(8,128)}, /*index=5*/f32[16]{0:T(128)S(1)}, s32[]{:T(128)}) while((s32[]{:T(128)}, f32[8,16,128,128]{3,2,1,0:T(8,128)}, s32[8,16,2]{1,0,2:T(8,128)S(1)}, f32[16,128,1024]{2,1,0:T(8,128)}, ...), condition=%wide.region_2.3_spmd, body=%wide.region_1.2_spmd.sunk | while | flops 3221489920 | bytes 51390416 | solution.py:32
  223.3 7.7 %gather_fusion = f32[16,128,1024]{2,1,0:T(8,128)} fusion(f32[16,128,1024]{2,1,0:T(8,128)} %get-tuple-element.128, s32[1024]{0:T(1024)S(1)} %get-tuple-element.109), kind=kCustom, calls=%fused_computation.clone.1 | custom fusion | bytes 16777280 | tf_op jit(solution)/shard_map/while/body/eval_jaxpr/gather | solution.py:19
  231.0 7.7 %gather_fusion.1 = f32[16,128,1024]{2,1,0:T(8,128)} fusion(f32[16,128,1024]{2,1,0:T(8,128)} %get-tuple-element.129, s32[1024]{0:T(1024)S(1)} %get-tuple-element.110), kind=kCustom, calls=%fused_computation.1.clone.1 | custom fusion | bytes 16777280 | tf_op jit(solution)/shard_map/while/body/eval_jaxpr/gather | solution.py:20
  238.7 12.4 %fusion.13 = f32[8,16,128,128]{3,2,1,0:T(8,128)} fusion(f32[8,16,128,128]{3,2,1,0:T(8,128)} %get-tuple-element.119, s32[]{:T(128)} %get-tuple-element.118, f32[16,128,1024]{2,1,0:T(8,128)} %gather_fusion, f32[16,128,1024]{2,1,0:T(8,128)} %gather_fusion.1, f32[16]{0:T(128)S(1)} %multiply_multiply_fusion.2), kind=kOutput, calls=%fused_computation.6.clone.1 | convolution fusion | flops 3221487616 | bytes 17826368 | tf_op jit(solution)/shard_map/while/body/eval_jaxpr/pao,pbo->pab/dot_general | solution.py:17
  252.5 7.7 %gather_fusion = f32[16,128,1024]{2,1,0:T(8,128)} fusion(f32[16,128,1024]{2,1,0:T(8,128)} %get-tuple-element.128, s32[1024]{0:T(1024)S(1)} %get-tuple-element.109), kind=kCustom, calls=%fused_computation.clone.1 | custom fusion | bytes 16777280 | tf_op jit(solution)/shard_map/while/body/eval_jaxpr/gather | solution.py:19
  267.9 12.5 %fusion.13 = f32[8,16,128,128]{3,2,1,0:T(8,128)} fusion(f32[8,16,128,128]{3,2,1,0:T(8,128)} %get-tuple-element.119, s32[]{:T(128)} %get-tuple-element.118, f32[16,128,1024]{2,1,0:T(8,128)} %gather_fusion, f32[16,128,1024]{2,1,0:T(8,128)} %gather_fusion.1, f32[16]{0:T(128)S(1)} %multiply_multiply_fusion.2), kind=kOutput, calls=%fused_computation.6.clone.1 | convolution fusion | flops 3221487616 | bytes 17826368 | tf_op jit(solution)/shard_map/while/body/eval_jaxpr/pao,pbo->pab/dot_general | solution.py:17
  281.7 7.7 %gather_fusion = f32[16,128,1024]{2,1,0:T(8,128)} fusion(f32[16,128,1024]{2,1,0:T(8,128)} %get-tuple-element.128, s32[1024]{0:T(1024)S(1)} %get-tuple-element.109), kind=kCustom, calls=%fused_computation.clone.1 | custom fusion | bytes 16777280 | tf_op jit(solution)/shard_map/while/body/eval_jaxpr/gather | solution.py:19
  297.1 12.4 %fusion.13 = f32[8,16,128,128]{3,2,1,0:T(8,128)} fusion(f32[8,16,128,128]{3,2,1,0:T(8,128)} %get-tuple-element.119, s32[]{:T(128)} %get-tuple-element.118, f32[16,128,1024]{2,1,0:T(8,128)} %gather_fusion, f32[16,128,1024]{2,1,0:T(8,128)} %gather_fusion.1, f32[16]{0:T(128)S(1)} %multiply_multiply_fusion.2), kind=kOutput, calls=%fused_computation.6.clone.1 | convolution fusion | flops 3221487616 | bytes 17826368 | tf_op jit(solution)/shard_map/while/body/eval_jaxpr/pao,pbo->pab/dot_general | solution.py:17
  310.9 7.7 %gather_fusion = f32[16,128,1024]{2,1,0:T(8,128)} fusion(f32[16,128,1024]{2,1,0:T(8,128)} %get-tuple-element.128, s32[1024]{0:T(1024)S(1)} %get-tuple-element.109), kind=kCustom, calls=%fused_computation.clone.1 | custom fusion | bytes 16777280 | tf_op jit(solution)/shard_map/while/body/eval_jaxpr/gather | solution.py:19
  326.3 12.5 %fusion.13 = f32[8,16,128,128]{3,2,1,0:T(8,128)} fusion(f32[8,16,128,128]{3,2,1,0:T(8,128)} %get-tuple-element.119, s32[]{:T(128)} %get-tuple-element.118, f32[16,128,1024]{2,1,0:T(8,128)} %gather_fusion, f32[16,128,1024]{2,1,0:T(8,128)} %gather_fusion.1, f32[16]{0:T(128)S(1)} %multiply_multiply_fusion.2), kind=kOutput, calls=%fused_computation.6.clone.1 | convolution fusion | flops 3221487616 | bytes 17826368 | tf_op jit(solution)/shard_map/while/body/eval_jaxpr/pao,pbo->pab/dot_general | solution.py:17
  340.1 7.7 %gather_fusion = f32[16,128,1024]{2,1,0:T(8,128)} fusion(f32[16,128,1024]{2,1,0:T(8,128)} %get-tuple-element.128, s32[1024]{0:T(1024)S(1)} %get-tuple-element.109), kind=kCustom, calls=%fused_computation.clone.1 | custom fusion | bytes 16777280 | tf_op jit(solution)/shard_map/while/body/eval_jaxpr/gather | solution.py:19
  355.5 12.4 %fusion.13 = f32[8,16,128,128]{3,2,1,0:T(8,128)} fusion(f32[8,16,128,128]{3,2,1,0:T(8,128)} %get-tuple-element.119, s32[]{:T(128)} %get-tuple-element.118, f32[16,128,1024]{2,1,0:T(8,128)} %gather_fusion, f32[16,128,1024]{2,1,0:T(8,128)} %gather_fusion.1, f32[16]{0:T(128)S(1)} %multiply_multiply_fusion.2), kind=kOutput, calls=%fused_computation.6.clone.1 | convolution fusion | flops 3221487616 | bytes 17826368 | tf_op jit(solution)/shard_map/while/body/eval_jaxpr/pao,pbo->pab/dot_general | solution.py:17
  369.3 7.7 %gather_fusion = f32[16,128,1024]{2,1,0:T(8,128)} fusion(f32[16,128,1024]{2,1,0:T(8,128)} %get-tuple-element.128, s32[1024]{0:T(1024)S(1)} %get-tuple-element.109), kind=kCustom, calls=%fused_computation.clone.1 | custom fusion | bytes 16777280 | tf_op jit(solution)/shard_map/while/body/eval_jaxpr/gather | solution.py:19
  384.7 12.4 %fusion.13 = f32[8,16,128,128]{3,2,1,0:T(8,128)} fusion(f32[8,16,128,128]{3,2,1,0:T(8,128)} %get-tuple-element.119, s32[]{:T(128)} %get-tuple-element.118, f32[16,128,1024]{2,1,0:T(8,128)} %gather_fusion, f32[16,128,1024]{2,1,0:T(8,128)} %gather_fusion.1, f32[16]{0:T(128)S(1)} %multiply_multiply_fusion.2), kind=kOutput, calls=%fused_computation.6.clone.1 | convolution fusion | flops 3221487616 | bytes 17826368 | tf_op jit(solution)/shard_map/while/body/eval_jaxpr/pao,pbo->pab/dot_general | solution.py:17
  398.4 7.7 %gather_fusion = f32[16,128,1024]{2,1,0:T(8,128)} fusion(f32[16,128,1024]{2,1,0:T(8,128)} %get-tuple-element.128, s32[1024]{0:T(1024)S(1)} %get-tuple-element.109), kind=kCustom, calls=%fused_computation.clone.1 | custom fusion | bytes 16777280 | tf_op jit(solution)/shard_map/while/body/eval_jaxpr/gather | solution.py:19
  413.8 12.4 %fusion.13 = f32[8,16,128,128]{3,2,1,0:T(8,128)} fusion(f32[8,16,128,128]{3,2,1,0:T(8,128)} %get-tuple-element.119, s32[]{:T(128)} %get-tuple-element.118, f32[16,128,1024]{2,1,0:T(8,128)} %gather_fusion, f32[16,128,1024]{2,1,0:T(8,128)} %gather_fusion.1, f32[16]{0:T(128)S(1)} %multiply_multiply_fusion.2), kind=kOutput, calls=%fused_computation.6.clone.1 | convolution fusion | flops 3221487616 | bytes 17826368 | tf_op jit(solution)/shard_map/while/body/eval_jaxpr/pao,pbo->pab/dot_general | solution.py:17
  427.6 7.7 %gather_fusion = f32[16,128,1024]{2,1,0:T(8,128)} fusion(f32[16,128,1024]{2,1,0:T(8,128)} %get-tuple-element.128, s32[1024]{0:T(1024)S(1)} %get-tuple-element.109), kind=kCustom, calls=%fused_computation.clone.1 | custom fusion | bytes 16777280 | tf_op jit(solution)/shard_map/while/body/eval_jaxpr/gather | solution.py:19
  443.0 12.4 %fusion.13 = f32[8,16,128,128]{3,2,1,0:T(8,128)} fusion(f32[8,16,128,128]{3,2,1,0:T(8,128)} %get-tuple-element.119, s32[]{:T(128)} %get-tuple-element.118, f32[16,128,1024]{2,1,0:T(8,128)} %gather_fusion, f32[16,128,1024]{2,1,0:T(8,128)} %gather_fusion.1, f32[16]{0:T(128)S(1)} %multiply_multiply_fusion.2), kind=kOutput, calls=%fused_computation.6.clone.1 | convolution fusion | flops 3221487616 | bytes 17826368 | tf_op jit(solution)/shard_map/while/body/eval_jaxpr/pao,pbo->pab/dot_general | solution.py:17
  455.5 148.9 %reduce-scatter.3.cloned.1.call-done = f32[2,128,128]{2,1,0:T(8,128)} async-done(((f32[128,128,128]{2,1,0:T(8,128)}), f32[2,128,128]{2,1,0:T(8,128)}) %reduce-scatter.3.cloned.1.call-update) | async-done | bytes 131088 | tf_op jit(solution)/shard_map/reduce_scatter | solution.py:52
  604.5 21.9 %reduce-scatter.5.cloned.1.call-done = f32[2,32,128]{2,1,0:T(8,128)} async-done(((f32[2,128,128]{2,1,0:T(8,128)}), f32[2,32,128]{2,1,0:T(8,128)}) %reduce-scatter.5.cloned.1.call-update) | async-done | bytes 32784 | tf_op jit(solution)/shard_map/reduce_scatter | solution.py:53
  (72 shorter events, 64.9 us)
Async XLA Ops:
  14.8 12.6 %copy-start.2 = (f32[16]{0:T(128)S(1)}, f32[16]{0:T(128)}, u32[]{:S(2)}) copy-start(f32[16]{0:T(128)} %param.9) | copy-start | bytes 196
  14.8 12.6 %copy-start.1 = (s32[128,2]{0,1:T(2,128)S(1)}, s32[128,2]{0,1:T(2,128)}, u32[]{:S(2)}) copy-start(s32[128,2]{0,1:T(2,128)} %param.11) | copy-start | bytes 3076
  14.8 12.7 %copy-start = (s32[1,1024]{1,0:T(1,128)S(1)}, s32[1,1024]{1,0:T(1,128)}, u32[]{:S(2)}) copy-start(s32[1,1024]{1,0:T(1,128)} %param.8) | copy-start | bytes 12292
  14.8 12.8 %copy-start.3 = (s32[1,1,16]{2,1,0:T(1,128)S(1)}, s32[1,1,16]{2,1,0:T(1,128)}, u32[]{:S(2)}) copy-start(s32[1,1,16]{2,1,0:T(1,128)} %param.10) | copy-start | bytes 196
  14.8 198.6 %all-to-all-start = ((f32[32,64,1024]{2,0,1:T(8,128)}), f32[32,64,1024]{2,0,1:T(8,128)}, u32[]{:S(2)}, u32[]{:S(2)}) async-start(f32[32,64,1024]{2,0,1:T(8,128)} %bitcast.36), calls=%async_computation | async-start | bytes 16777216 | tf_op jit(solution)/shard_map/all_to_all | solution.py:39
  27.3 577.1 %reduce-scatter.3.cloned.1.call-start = ((), (), s32[]{:S(2)}) async-start(), calls=%async_computation.3 | async-start | bytes 8519680 | tf_op jit(solution)/shard_map/reduce_scatter | solution.py:52
  455.5 170.9 %reduce-scatter.5.cloned.1.call-start = ((), (), s32[]{:S(2)}) async-start(), calls=%async_computation.4 | async-start | bytes 163840 | tf_op jit(solution)/shard_map/reduce_scatter | solution.py:53
Sparse Core Ops, SparseCore 0:
  455.6 148.8 reduce-scatter.2
  607.1 19.2 reduce-scatter.4
where the time goes:
time: 636 us; the launch traced here: 633 us
  waiting for transfers between devices  357 us (56%)
  local copies, waits for them, and re-layouts  142 us (22%)
  matrix products  99.5 us (16%)
  between operations  13.5 us (2%)
  starting transfers between devices  12.6 us (2%)
  other arithmetic  8.83 us (1%)
    all_to_all x1, waiting for transfers between devices, on_device(): lax.all_to_all(jac_cols, 'obs', split_axis=1, concat_axis=0, tiled=True)  186 us
    reduce_scatter x1, waiting for transfers between devices, on_device(): owned = lax.psum_scatter(run(pairs), 'obs', scatter_dimension=0, tiled=True)  149 us
    dot_general x8, matrix products, group_tiles(): jnp.einsum('pao,pbo->pab', jblocks[first], wblocks[second], precision=lax...  99.5 us
    gather x8, local copies, waits for them, and re-layouts, group_tiles(): jblocks[first]  61.6 us
    gather x8, local copies, waits for them, and re-layouts, group_tiles(): wblocks[second]  61.5 us
    reduce_scatter x1, waiting for transfers between devices, on_device(): return lax.psum_scatter(owned, 'blk', scatter_dimension=1, tiled=True)  21.9 us
  transfers between devices with their start and end apart: 3, of which 3 were waited for; matrix products, arithmetic and copies ran while one was open for 0% of the time, Pallas kernels for 0%

commit v1 on v0

v1 whole, which is shorter than its diff:
```python
import math

import jax
import jax.numpy as jnp
import numpy as np
from jax import lax
from jax.experimental import pallas as pl
from jax.experimental.pallas import tpu as pltpu
from jax.sharding import Mesh, PartitionSpec as P

NZ, NY, NC, NX = 8, 4, 2, 4
OBS_AXES = ("z", "y", "c")
VMEM_LIMIT = 60 * 1024 * 1024


def relayout(jac):
    rows, total = jac.shape
    parts = NZ * NY * NC
    width = total // parts
    step = NY * NC

    def body(src, dst):
        for s in range(step):
            dst[s] = src[:, s * width:(s + 1) * width]

    return pl.pallas_call(
        body,
        grid=(parts // step,),
        in_specs=[pl.BlockSpec((rows, step * width), lambda i: (0, i))],
        out_specs=pl.BlockSpec((step, rows, width), lambda i: (i, 0, 0)),
        out_shape=jax.ShapeDtypeStruct((parts, rows, width), jac.dtype),
        name="relayout",
    )(jac)


def super_tiles(groups, zs, info, factors):
    count = len(groups)
    width = groups[0].shape[-1]
    pairs = info["pairs"]
    npair = len(pairs)
    first = jnp.stack([zs[a] for a, _ in pairs])
    second = jnp.stack([zs[b] for _, b in pairs])
    slot_a = jnp.array([a for a, _ in pairs], jnp.int32)
    slot_b = jnp.array([b for _, b in pairs], jnp.int32)
    swap = first > second
    rows = jnp.where(swap, slot_b, slot_a)
    cols = jnp.where(swap, slot_a, slot_b)
    core = lax.axis_index("c").astype(jnp.int32).reshape(1)

    def body(rows_ref, cols_ref, core_ref, *refs):
        srcs = refs[:count]
        fac = refs[count]
        keep, give = refs[count + 1:count + 3]
        high, low, acc = refs[count + 3:]
        step = pl.program_id(0)

        @pl.when(step == 0)
        def _():
            for g in range(count):

                def split(s, carry, g=g):
                    half = s // (NY * NC // 2)
                    value = srcs[g][s] * fac[pl.ds(2 * g + half, 1), :]
                    top = value.astype(jnp.bfloat16)
                    rest = (value - top.astype(jnp.float32)).astype(jnp.bfloat16)
                    start = pl.multiple_of(s * 32, 32)
                    high[g, pl.ds(start, 32), :] = top
                    low[g, pl.ds(start, 32), :] = rest
                    return carry

                lax.fori_loop(0, NY * NC, split, 0)

        a = rows_ref[step]
        b = cols_ref[step]

        def dot(u, v):
            return lax.dot_general(
                u, v, (((1,), (1,)), ((), ())), preferred_element_type=jnp.float32
            )

        ha, hb = high[a], high[b]
        acc[...] = dot(ha, hb) + (dot(ha, low[b]) + dot(low[a], hb))
        mine = core_ref[0]
        for x in range(NX):
            for y in range(NY):
                at = x * 32 + y * 8
                own = pl.multiple_of(mine * 128 + at, 8)
                other = pl.multiple_of((1 - mine) * 128 + at, 8)
                for h in range(2):
                    lanes = slice(h * 128, (h + 1) * 128)
                    keep[y, x, 0, h] = acc[pl.ds(own, 8), lanes]
                    give[y, x, 0, h] = acc[pl.ds(other, 8), lanes]

    shape = (NY, NX, npair, 2, 8, 128)
    block = pl.BlockSpec((NY, NX, 1, 2, 8, 128), lambda p, *_: (0, 0, p, 0, 0, 0))
    whole = pl.BlockSpec((NY * NC, 32, width), lambda p, *_: (0, 0, 0))
    return pl.pallas_call(
        body,
        grid_spec=pltpu.PrefetchScalarGridSpec(
            num_scalar_prefetch=3,
            grid=(npair,),
            in_specs=[whole] * count
            + [pl.BlockSpec((2 * count, width), lambda p, *_: (0, 0))],
            out_specs=[block, block],
            scratch_shapes=[
                pltpu.VMEM((count, 256, width), jnp.bfloat16),
                pltpu.VMEM((count, 256, width), jnp.bfloat16),
                pltpu.VMEM((256, 256), jnp.float32),
            ],
        ),
        out_shape=[jax.ShapeDtypeStruct(shape, jnp.float32)] * 2,
        compiler_params=pltpu.CompilerParams(vmem_limit_bytes=VMEM_LIMIT),
        cost_estimate=pl.CostEstimate(
            flops=npair * 256 * 256 * width * 6,
            bytes_accessed=count * 256 * width * 4 + npair * 256 * 256 * 4,
            transcendentals=0,
        ),
        name="super_tiles",
    )(rows, cols, core, *groups, factors)


def swap_cores(value):
    return lax.ppermute(value, "c", [(0, 1), (1, 0)])


def reduce_rows(keep, give):
    total = keep + swap_cores(give)
    parts = total.reshape(NY * NX, -1, 8, 128)
    return lax.all_to_all(parts, ("y", "x"), 0, 0, tiled=True)


def gather_tiles(parts, index, valid):
    sizes = [p.shape[1] for p in parts]
    count = index.shape[0]

    def body(index_ref, valid_ref, *refs):
        srcs = refs[:len(parts)]
        out, sums = refs[len(parts):]
        base = 0
        for src, size in zip(srcs, sizes):

            def add(t, carry, src=src, base=base):
                value = src[0, t]
                for s in range(1, NY * NX):
                    value = value + src[s, t]
                sums[base + t] = value
                return carry

            lax.fori_loop(0, size, add, 0)
            base += size

        def pick(k, carry):
            value = sums[index_ref[k]]
            out[k] = jnp.where(valid_ref[k] > 0, value, 0.0)
            return carry

        lax.fori_loop(0, count, pick, 0)

    return pl.pallas_call(
        body,
        grid_spec=pltpu.PrefetchScalarGridSpec(
            num_scalar_prefetch=2,
            grid=(1,),
            in_specs=[pl.BlockSpec(p.shape, lambda i, *_: (0, 0, 0, 0)) for p in parts],
            out_specs=pl.BlockSpec((count, 8, 128), lambda i, *_: (0, 0, 0)),
            scratch_shapes=[pltpu.VMEM((sum(sizes), 8, 128), jnp.float32)],
        ),
        out_shape=jax.ShapeDtypeStruct((count, 8, 128), jnp.float32),
        compiler_params=pltpu.CompilerParams(vmem_limit_bytes=VMEM_LIMIT),
        name="gather_tiles",
    )(index, valid, *parts)


def on_device(jac, obs_group, group_weight, pattern, pairs):
    count = pairs.shape[0]
    total_obs = jac.shape[1] * NX
    message = relayout(jac)
    received = lax.all_to_all(message, OBS_AXES, 0, 0, tiled=True)
    groups = [received[g * NY * NC:(g + 1) * NY * NC] for g in range(NZ)]
    zs = [jnp.int32(g) for g in range(NZ)]

    choice = obs_group[0][None, :] == jnp.arange(group_weight.shape[0], dtype=jnp.int32)[:, None]
    root = jnp.sum(jnp.where(choice, group_weight[:, None], 0.0), axis=0)
    factors = pattern[0, 0].astype(jnp.float32)[:, None] * root[None, :]

    listed = [(a, b) for a in range(NZ) for b in range(a, NZ)]
    table = np.zeros((NZ, NZ), np.int32)
    for at, (a, b) in enumerate(listed):
        table[a, b] = table[b, a] = at
    keep, give = super_tiles(groups, zs, {"pairs": listed}, factors)
    part = reduce_rows(keep, give)

    first, second = pairs[:, 0], pairs[:, 1]
    place = jnp.asarray(table)[first // 2, second // 2] * 2 + second % 2
    valid = (first % 2 == lax.axis_index("c")).astype(jnp.int32)
    tiles = gather_tiles([part], place, valid)
    owned = lax.all_to_all(
        tiles.reshape(NZ * NY * NC, count // (NZ * NY * NC), 8, 128), OBS_AXES, 0, 0, tiled=True
    )
    owned = owned.reshape(NZ, NY, NC, -1, 8, 128)
    result = jnp.sum(owned, axis=(0, 2)) * (1.0 / math.sqrt(total_obs))
    return result.transpose(1, 0, 2, 3).reshape(-1, NY * 8, 128)


def solution(mesh):
    fine = Mesh(mesh.devices.reshape(NZ, NY, NC, NX), ("z", "y", "c", "x"))
    return jax.shard_map(
        on_device,
        mesh=fine,
        in_specs=(P(OBS_AXES, "x"), P("x", OBS_AXES), P(), P("x", OBS_AXES, None), P()),
        out_specs=P(OBS_AXES, "x", None),
        check_vma=False,
    )
```

time: 636 us -> 369 us (0.58)
  local copies, waits for them, and re-layouts: 142 us -> 7.89 us
  matrix products: 99.5 us -> 0 us
  waiting for transfers between devices: 357 us -> 261 us
  Pallas kernels: 0 us -> 46.8 us
  blocking collectives: 0 us -> 23.7 us
  between operations: 13.5 us -> 0.09 us
  starting transfers between devices: 12.6 us -> 20.2 us
    reduce_scatter x2 -> x0, waiting for transfers between devices: 171 us -> none  [the longest x1 149 us: on_device(): owned = lax.psum_scatter(run(pairs), 'obs', scatter_dimension=0, tiled=True)]
    gather x32 -> x1, local copies, waits for them, and re-layouts: 134 us -> 1 us  [on_device(): place = jnp.asarray(table)[first // 2, second // 2] * 2 + second % 2]
    dot_general x8 -> x0, matrix products: 99.5 us -> none  [group_tiles(): jnp.einsum('pao,pbo->pab', jblocks[first], wblocks[second], precision=lax...]
    all_to_all x1 -> x2, waiting for transfers between devices: 186 us -> 252 us  [the longest x1 185 us: on_device(): received = lax.all_to_all(message, OBS_AXES, 0, 0, tiled=True)]
    pallas_call x0 -> x3, Pallas kernels: none -> 46.8 us  [the longest x1 31.9 us: super_tiles(): pl.pallas_call(body, grid_spec=pltpu.PrefetchScalarGridSpec(num_scalar_pr...]
    all_to_all x0 -> x1, blocking collectives: none -> 23.7 us  [on_device(): lax.all_to_all(tiles.reshape(NZ * NY * NC, count // (NZ * NY * NC), 8, 12...]
    all_to_all x1 -> x0, local copies, waits for them, and re-layouts: 8.27 us -> none  [on_device(): lax.all_to_all(jac_cols, 'obs', split_axis=1, concat_axis=0, tiled=True)]
    ppermute x0 -> x1, waiting for transfers between devices: none -> 8.12 us  [swap_cores(): return lax.ppermute(value, 'c', [(0, 1), (1, 0)])]
  transfers between devices with their start and end apart: 3 -> 3, of which waited for: 3 -> 3; matrix products, arithmetic and copies ran while one was open for 0% -> 1% of each run, Pallas kernels for 0% -> 0%
where the time goes in v1:
time: 369 us; the launch traced here: 367 us
  waiting for transfers between devices  261 us (71%)
  Pallas kernels  46.8 us (13%)
  blocking collectives  23.7 us (6%)
  starting transfers between devices  20.2 us (5%)
  local copies, waits for them, and re-layouts  7.89 us (2%)
  other arithmetic  7.69 us (2%)
    all_to_all x1, waiting for transfers between devices, on_device(): received = lax.all_to_all(message, OBS_AXES, 0, 0, tiled=True)  185 us
    all_to_all x1, waiting for transfers between devices, reduce_rows(): return lax.all_to_all(parts, ('y', 'x'), 0, 0, tiled=True)  67.2 us
    pallas_call x1, Pallas kernels, super_tiles(): pl.pallas_call(body, grid_spec=pltpu.PrefetchScalarGridSpec(num_scalar_pr...  31.9 us
    all_to_all x1, blocking collectives, on_device(): lax.all_to_all(tiles.reshape(NZ * NY * NC, count // (NZ * NY * NC), 8, 12...  23.7 us
    all_to_all x1, starting transfers between devices, on_device(): received = lax.all_to_all(message, OBS_AXES, 0, 0, tiled=True)  12.5 us
    pallas_call x1, Pallas kernels, relayout(): pl.pallas_call(body, grid=(parts // step,), in_specs=[pl.BlockSpec((rows,...  8.96 us
    ppermute x1, waiting for transfers between devices, swap_cores(): return lax.ppermute(value, 'c', [(0, 1), (1, 0)])  8.12 us
    all_to_all x1, starting transfers between devices, reduce_rows(): return lax.all_to_all(parts, ('y', 'x'), 0, 0, tiled=True)  7.7 us
  transfers between devices with their start and end apart: 3, of which 3 were waited for; matrix products, arithmetic and copies ran while one was open for 1% of the time, Pallas kernels for 0%

profile of v1, /device:TPU:6, one launch (start us, length us, event | category | flops | bytes accessed | tf_op | source)
XLA Modules:
  0.0 367.0 jit_solution(10832688591675977892)
XLA Ops:
  0.0 9.0 %relayout.1 = f32[64,32,1024]{2,1,0:T(8,128)} custom-call(f32[32,65536]{1,0:T(8,128)} %src.1), custom_call_target="tpu_custom_call" | custom-call | tf_op jit(solution)/shard_map/relayout/pallas_call | solution.py:26
  9.0 0.0 copy-start.2
  9.0 12.5 %all-to-all-start = ((f32[64,32,1024]{2,1,0:T(8,128)}), f32[64,32,1024]{2,1,0:T(8,128)}, u32[]{:S(2)}, u32[]{:S(2)}) async-start(f32[64,32,1024]{2,1,0:T(8,128)} %relayout.1), calls=%async_computation | async-start | bytes 16777216 | tf_op jit(solution)/shard_map/all_to_all | solution.py:178
  21.5 0.0 copy-done.1
  21.5 0.0 copy-done.2
  21.5 0.1 select_reduce_fusion
  21.6 0.0 copy-done.4
  21.6 0.7 broadcast_multiply_fusion.refs_8_
  22.3 185.2 %all-to-all-done = f32[64,32,1024]{2,1,0:T(8,128)} async-done(((f32[64,32,1024]{2,1,0:T(8,128)}), f32[64,32,1024]{2,1,0:T(8,128)}, u32[]{:S(2)}, u32[]{:S(2)}) %all-to-all-start) | async-done | bytes 8388640 | tf_op jit(solution)/shard_map/all_to_all | solution.py:178
  207.5 6.9 %fusion.9 = (f32[8,32,1024]{2,1,0:T(8,128)}, f32[8,32,1024]{2,1,0:T(8,128)}, f32[8,32,1024]{2,1,0:T(8,128)}, f32[8,32,1024]{2,1,0:T(8,128)}, f32[8,32,1024]{2,1,...) fusion(f32[64,32,1024]{2,1,0:T(8,128)} %all-to-all-done), kind=kLoop, calls=%fused_computation.33 | loop fusion | bytes 16777216 | tf_op jit(solution)/shard_map/slice | solution.py:179
  214.4 31.9 %super_tiles.1 = (f32[4,4,36,2,8,128]{5,4,3,2,1,0:T(8,128)}, f32[4,4,36,2,8,128]{5,4,3,2,1,0:T(8,128)}) custom-call(s32[36]{0:T(128)} %constant.59.clone.rows_ref, s32[36]{0:T(128)} %constant.60.clone.cols_ref, s32[1]{0:T(128)} %bitcast.3.core_ref, f32[8,32,1024]{2,1,0:T(8,128)} %get-tuple-element.16.refs_0_, f32[8,32,1024]{2,1,0:T(8,128)} %get-tuple-element.15.refs_1_, ...), custom_call_target="tpu_custom_call" | custom-call | flops 14495514624 | bytes 17825792 | tf_op jit(solution)/shard_map/super_tiles/pallas_call | solution.py:97
  246.3 0.0 collective-permute-start
  246.3 8.1 %collective-permute-done = f32[4,4,36,2,8,128]{5,4,3,2,1,0:T(8,128)S(1)} collective-permute-done((f32[4,4,36,2,8,128]{5,4,3,2,1,0:T(8,128)}, f32[4,4,36,2,8,128]{5,4,3,2,1,0:T(8,128)S(1)}, u32[]{:S(2)}, u32[]{:S(2)}) %collective-permute-start) | collective-permute-done | bytes 4718624 | tf_op jit(solution)/shard_map/ppermute | solution.py:123
  254.4 5.1 %add.33 = f32[4,4,36,2,8,128]{5,4,3,2,1,0:T(8,128)} add(f32[4,4,36,2,8,128]{5,4,3,2,1,0:T(8,128)} %get-tuple-element.7, f32[4,4,36,2,8,128]{5,4,3,2,1,0:T(8,128)S(1)} %collective-permute-done) | non-fusion elementwise | flops 1179648 | bytes 14155776 | tf_op jit(solution)/shard_map/add | solution.py:127
  259.5 7.7 %all-to-all-start.1 = ((f32[16,72,8,128]{3,2,1,0:T(8,128)}), f32[16,72,8,128]{3,2,1,0:T(8,128)}, u32[]{:S(2)}, u32[]{:S(2)}) async-start(f32[16,72,8,128]{3,2,1,0:T(8,128)} %bitcast.18), calls=%async_computation.1 | async-start | bytes 9437184 | tf_op jit(solution)/shard_map/all_to_all | solution.py:129
  267.2 0.0 copy-done.3
  267.3 0.0 copy-done
  267.3 1.0 gather_fusion
  268.3 0.6 compare_convert_fusion.valid_ref
  268.9 0.5 fusion.index_ref
  269.4 67.2 %all-to-all-done.1.refs_0_ = f32[16,72,8,128]{3,2,1,0:T(8,128)} async-done(((f32[16,72,8,128]{3,2,1,0:T(8,128)}), f32[16,72,8,128]{3,2,1,0:T(8,128)}, u32[]{:S(2)}, u32[]{:S(2)}) %all-to-all-start.1) | async-done | bytes 4718624 | tf_op jit(solution)/shard_map/all_to_all | solution.py:129
  336.6 6.0 %gather_tiles.1 = f32[128,8,128]{2,1,0:T(8,128)} custom-call(s32[128]{0:T(128)} %fusion.index_ref, s32[128]{0:T(128)} %compare_convert_fusion.valid_ref, f32[16,72,8,128]{3,2,1,0:T(8,128)} %all-to-all-done.1.refs_0_), custom_call_target="tpu_custom_call" | custom-call | tf_op jit(solution)/shard_map/gather_tiles/pallas_call | solution.py:159
  342.6 23.7 %all_to_all.15 = f32[64,2,8,128]{3,2,1,0:T(8,128)S(1)} all-to-all(f32[64,2,8,128]{3,2,1,0:T(8,128)} %bitcast.20), channel_id=1, replica_groups=mesh['z'=8,'y'=4,'c'=2,'x'=4] {'z','y','c'}, dimensions={0} | all-to-all | bytes 1048576 | tf_op jit(solution)/shard_map/all_to_all | solution.py:197
  366.3 0.6 copy_bitcast_fusion
  (7 shorter events, 0.1 us)
Async XLA Ops:
  9.0 12.5 %copy-start.1 = (s32[1,1024]{1,0:T(1,128)S(1)}, s32[1,1024]{1,0:T(1,128)}, u32[]{:S(2)}) copy-start(s32[1,1024]{1,0:T(1,128)} %param.9) | copy-start | bytes 12292
  9.0 12.5 %copy-start.2 = (f32[16]{0:T(128)S(1)}, f32[16]{0:T(128)}, u32[]{:S(2)}) copy-start(f32[16]{0:T(128)} %param.10) | copy-start | bytes 196
  9.0 12.6 %copy-start.4 = (s32[1,1,16]{2,1,0:T(1,128)S(1)}, s32[1,1,16]{2,1,0:T(1,128)}, u32[]{:S(2)}) copy-start(s32[1,1,16]{2,1,0:T(1,128)} %param.11) | copy-start | bytes 196
  9.0 198.6 %all-to-all-start = ((f32[64,32,1024]{2,1,0:T(8,128)}), f32[64,32,1024]{2,1,0:T(8,128)}, u32[]{:S(2)}, u32[]{:S(2)}) async-start(f32[64,32,1024]{2,1,0:T(8,128)} %relayout.1), calls=%async_computation | async-start | bytes 16777216 | tf_op jit(solution)/shard_map/all_to_all | solution.py:178
  246.3 8.1 %collective-permute-start = (f32[4,4,36,2,8,128]{5,4,3,2,1,0:T(8,128)}, f32[4,4,36,2,8,128]{5,4,3,2,1,0:T(8,128)S(1)}, u32[]{:S(2)}, u32[]{:S(2)}) collective-permute-start(f32[4,4,36,2,8,128]{5,4,3,2,1,0:T(8,128)} %get-tuple-element.8), channel_id=1, source_target_pairs={{0,4},{4,0},{1,5},{5,1},{2,6},{6,2},{3,7},{7,3},{8,12},{12,8},{9,1... | collective-permute-start | bytes 14155784 | tf_op jit(solution)/shard_map/ppermute | solution.py:123
  259.5 7.7 %copy-start.3 = (s32[128,2]{0,1:T(2,128)S(1)}, s32[128,2]{0,1:T(2,128)}, u32[]{:S(2)}) copy-start(s32[128,2]{0,1:T(2,128)} %param.12) | copy-start | bytes 3076
  259.5 7.7 %copy-start = (s32[8,8]{1,0:T(8,128)S(1)}, s32[8,8]{1,0:T(8,128)}, u32[]{:S(2)}) copy-start(s32[8,8]{1,0:T(8,128)} %constant.61.clone) | copy-start | bytes 772
  259.5 77.1 %all-to-all-start.1 = ((f32[16,72,8,128]{3,2,1,0:T(8,128)}), f32[16,72,8,128]{3,2,1,0:T(8,128)}, u32[]{:S(2)}, u32[]{:S(2)}) async-start(f32[16,72,8,128]{3,2,1,0:T(8,128)} %bitcast.18), calls=%async_computation.1 | async-start | bytes 9437184 | tf_op jit(solution)/shard_map/all_to_all | solution.py:129

commit v2 on v0

v2 whole, which is shorter than its diff:
```python
import math

import jax
import jax.numpy as jnp
from jax import lax
from jax.experimental import pallas as pl
from jax.experimental.pallas import tpu as pltpu
from jax.sharding import Mesh, PartitionSpec as P

NZ, NY, NC, NX = 8, 4, 2, 4
PARTS = NZ * NY * NC
OBS_AXES = ("z", "y", "c")
NB, BS = 16, 128
OWNERS = 4
EARLY, LATE = 24, 8
EA, LA = OWNERS * EARLY, OWNERS * LATE
VMEM_LIMIT = 60 * 1024 * 1024
SMALL = pl.CostEstimate(flops=1, bytes_accessed=1, transcendentals=0)
PARAMS = pltpu.CompilerParams(vmem_limit_bytes=VMEM_LIMIT)
ANYWHERE = pl.BlockSpec(memory_space=pl.ANY)


def relayout(jac, start, rows):
    width = jac.shape[1] // PARTS

    def body(src, out, hold, sems):
        loads, stores = [], []
        for i in range(PARTS):
            part = src.at[pl.ds(start, rows), pl.ds(i * width, width)]
            loads.append(pltpu.make_async_copy(part, hold.at[i], sems.at[0, i]))
            stores.append(pltpu.make_async_copy(hold.at[i], out.at[i], sems.at[1, i]))
        for load in loads:
            load.start()
        for load, store in zip(loads, stores):
            load.wait()
            store.start()
        for store in stores:
            store.wait()

    shape = (PARTS, rows, width)
    return pl.pallas_call(
        body,
        in_specs=[ANYWHERE],
        out_specs=ANYWHERE,
        out_shape=jax.ShapeDtypeStruct(shape, jac.dtype),
        scratch_shapes=[pltpu.VMEM(shape, jac.dtype), pltpu.SemaphoreType.DMA((2, PARTS))],
        compiler_params=PARAMS,
        cost_estimate=SMALL,
        name="relayout",
    )(jac)


def dot(u, v):
    return lax.dot_general(u, v, (((1,), (1,)), ((), ())), preferred_element_type=jnp.float32)


def split(value):
    top = value.astype(jnp.bfloat16)
    return top, (value - top.astype(jnp.float32)).astype(jnp.bfloat16)


def each_pair(pairs_ref, mine, store):
    def one(s, carry):
        z, y, w = s // (NY * 2), (s // 2) % NY, s % 2
        k = ((z * NY + y) * NC + mine) * 2 + w
        store(y, z * 2 + w, pairs_ref[2 * k], pairs_ref[2 * k + 1])
        return carry

    lax.fori_loop(0, NZ * NY * 2, one, 0, unroll=8)


def early_tiles(received, factors, pairs, core):
    width = received.shape[-1]
    pieces = 4
    held = PARTS // pieces
    total = NB * EA
    tall = 256

    def body(pairs_ref, core_ref, fac, src, give, keep, kept, arrived, halves, prod, out, sems):
        loads = [
            pltpu.make_async_copy(
                src.at[pl.ds(p * held, held)], arrived.at[pl.ds(p * held, held)], sems.at[p]
            )
            for p in range(pieces)
        ]
        for load in loads:
            load.start()
        prod[:, total:] = jnp.zeros((total, BS), jnp.float32)

        def convert(i, carry):
            value = arrived[pl.ds(i * OWNERS, OWNERS)].reshape(EA, width) * fac[pl.ds(i, 1), :]
            rows = pl.ds(pl.multiple_of(i * EA, EA), EA)
            halves[0, rows, :], halves[1, rows, :] = split(value)
            return carry

        ready = 0
        for g in range(total // tall):
            while ready * held * EARLY < (g + 1) * tall:
                loads[ready].wait()
                lax.fori_loop(ready * held // OWNERS, (ready + 1) * held // OWNERS, convert, 0)
                ready += 1
            cols = slice(g * tall, (g + 1) * tall)

            def row(a, carry, cols=cols):
                rows = pl.ds(pl.multiple_of(a * tall, tall), tall)
                ah, al = halves[0, rows, :], halves[1, rows, :]
                bh, bl = halves[0, cols, :], halves[1, cols, :]
                prod[rows, cols] = dot(ah, bh) + (dot(ah, bl) + dot(al, bh))
                return carry

            lax.fori_loop(0, g + 1, row, 0)
            if g:
                rows, cols = slice(g * tall, g * tall + 64), slice(g * tall - BS, g * tall)
                ah, al = halves[0, rows, :], halves[1, rows, :]
                bh, bl = halves[0, cols, :], halves[1, cols, :]
                prod[rows, cols] = dot(ah, bh) + (dot(ah, bl) + dot(al, bh))

        save = pltpu.make_async_copy(halves, kept, sems.at[pieces])
        save.start()
        lane = lax.broadcasted_iota(jnp.int32, (EARLY, BS), 1)
        sends = []

        for n, (dst, who) in enumerate(((give, 1 - core_ref[0]), (keep, core_ref[0]))):

            def store(y, at, i, j, n=n):
                rows = pl.multiple_of(i * EA, EA)
                block = j * EA // BS
                skip = j * EA - block * BS
                back = lax.rem(BS - skip, BS)
                near = pl.ds(pl.multiple_of(block * BS, BS), BS)
                far = pl.ds(pl.multiple_of(block * BS + BS, BS), BS)
                for x in range(NX):
                    which = pl.ds(rows + x * EARLY, EARLY)
                    low = pltpu.roll(prod[which, near], back, 1)
                    high = pltpu.roll(prod[which, far], back, 1)
                    out[n, x, y, at] = jnp.where(lane < BS - skip, low, high)

            each_pair(pairs_ref, who, store)
            send = pltpu.make_async_copy(out.at[n], dst, sems.at[pieces + 1 + n])
            send.start()
            sends.append(send)
        for send in sends:
            send.wait()
        save.wait()

    shape = (NX, NY, NZ * 2, EARLY, BS)
    return pl.pallas_call(
        body,
        grid_spec=pltpu.PrefetchScalarGridSpec(
            num_scalar_prefetch=2,
            grid=(1,),
            in_specs=[pl.BlockSpec(factors.shape, lambda i, *_: (0, 0)), ANYWHERE],
            out_specs=[ANYWHERE] * 3,
            scratch_shapes=[
                pltpu.VMEM(received.shape, jnp.float32),
                pltpu.VMEM((2, total, width), jnp.bfloat16),
                pltpu.VMEM((total, total + BS), jnp.float32),
                pltpu.VMEM((2,) + shape, jnp.float32),
                pltpu.SemaphoreType.DMA((pieces + 3,)),
            ],
        ),
        out_shape=[jax.ShapeDtypeStruct(shape, jnp.float32)] * 2
        + [jax.ShapeDtypeStruct((2, total, width), jnp.bfloat16)],
        compiler_params=PARAMS,
        cost_estimate=pl.CostEstimate(flops=10**11, bytes_accessed=18 * 2**20, transcendentals=0),
        name="early_tiles",
    )(pairs, core, factors, received)


def late_tiles(received, kept, factors, pairs, core, *waited):
    width = received.shape[-1]

    def body(pairs_ref, core_ref, src, fac, kept_ref, *refs):
        refs = refs[len(waited):]
        keep, gives = refs[0], refs[1:1 + NX]
        halves, late, prod, out, sems = refs[1 + NX:]
        loads = [
            pltpu.make_async_copy(
                kept_ref.at[:, pl.ds(2 * g, 2)], halves.at[:, pl.ds(2 * g, 2), pl.ds(0, EA), :], sems.at[g]
            )
            for g in range(NB // 2)
        ]
        for load in loads:
            load.start()

        def convert(i, carry):
            value = src[pl.ds(i * OWNERS, OWNERS)].reshape(LA, width) * fac[pl.ds(i, 1), :]
            rows = pl.ds(pl.multiple_of(i * LA, LA), LA)
            for part, half in enumerate(split(value)):
                halves[part, i, EA:BS, :] = half
                late[part, rows, :] = half
            return carry

        lax.fori_loop(0, NB, convert, 0)

        def column(g, carry):
            for h in range(NB // 2):

                @pl.when(g == h)
                def _(h=h):
                    loads[h].wait()

            bh, bl = (halves[part, pl.ds(2 * g, 2)].reshape(2 * BS, width) for part in (0, 1))
            ah, al = late[0], late[1]
            cols = pl.ds(pl.multiple_of(g * 256, 256), 256)
            prod[:, cols] = dot(ah, bh) + (dot(ah, bl) + dot(al, bh))
            return carry

        lax.fori_loop(0, NB // 2, column, 0)
        lane = lax.broadcasted_iota(jnp.int32, (LATE, BS), 1)
        masks = {far: (lane // (far * EARLY)) % 2 == 0 for far in (2, 1)}

        sends = []

        for n, who in enumerate((1 - core_ref[0], core_ref[0])):

            def store(y, at, i, j, n=n):
                part = prod[pl.ds(pl.multiple_of(i * LA, LA), LA), pl.ds(pl.multiple_of(j * BS, BS), BS)]
                flip = prod[pl.ds(pl.multiple_of(j * LA, LA), LA), pl.ds(pl.multiple_of(i * BS, BS), BS)]
                turn = [flip[q * LATE:(q + 1) * LATE] for q in range(OWNERS)]
                for far in (2, 1):
                    by = far * EARLY
                    for q in range(OWNERS):
                        if q & far == 0:
                            u, v = turn[q], turn[q | far]
                            turn[q] = jnp.where(masks[far], u, pltpu.roll(v, by, 1))
                            turn[q | far] = jnp.where(masks[far], pltpu.roll(u, BS - by, 1), v)
                for x in range(NX):
                    out[n, x, y, at, 0:LATE] = part[x * LATE:(x + 1) * LATE]
                    out[n, x, y, at, LATE:2 * LATE] = turn[x]

            each_pair(pairs_ref, who, store)
            for x in range(NX):
                dst = keep.at[x] if n else gives[x]
                sends.append(pltpu.make_async_copy(out.at[n, x], dst, sems.at[NB // 2 + n * NX + x]))
                sends[-1].start()
        for send in sends:
            send.wait()

    shape = (NX, NY, NZ * 2, 2 * LATE, BS)
    whole = lambda shape: pl.BlockSpec(shape, lambda i, *_: (0,) * len(shape))
    return pl.pallas_call(
        body,
        grid_spec=pltpu.PrefetchScalarGridSpec(
            num_scalar_prefetch=2,
            grid=(1,),
            in_specs=[whole(received.shape), whole(factors.shape)] + [ANYWHERE] * (1 + len(waited)),
            out_specs=[ANYWHERE] * (1 + NX),
            scratch_shapes=[
                pltpu.VMEM((2, NB, BS, width), jnp.bfloat16),
                pltpu.VMEM((2, NB * LA, width), jnp.bfloat16),
                pltpu.VMEM((NB * LA, NB * BS), jnp.float32),
                pltpu.VMEM((2,) + shape, jnp.float32),
                pltpu.SemaphoreType.DMA((NB // 2 + 2 * NX,)),
            ],
        ),
        out_shape=[jax.ShapeDtypeStruct(shape, jnp.float32)]
        + [jax.ShapeDtypeStruct(shape[1:], jnp.float32)] * NX,
        compiler_params=PARAMS,
        cost_estimate=pl.CostEstimate(flops=10**11, bytes_accessed=12 * 2**20, transcendentals=0),
        name="late_tiles",
    )(pairs, core, received, factors, kept, *waited)


def swap_cores(value):
    return lax.ppermute(value, "c", [(0, 1), (1, 0)])


def total(axis, wholes, pieces, *waited):
    size = wholes[0].shape[0]
    shape = wholes[0].shape[1:]
    place = lax.axis_index(axis).astype(jnp.int32).reshape(1)

    def body(place_ref, *refs):
        whole_refs = refs[:len(wholes)]
        piece_refs = refs[len(wholes):len(wholes) + len(pieces)]
        outs = refs[len(refs) - size:]
        for d in range(size):
            at = lax.rem(place_ref[0] + d, size)
            for s in range(size):

                @pl.when(at == s)
                def _(d=d, s=s):
                    value = whole_refs[0][s]
                    for ref in whole_refs[1:]:
                        value = value + ref[s]
                    if pieces:
                        value = value + piece_refs[s][...]
                    outs[d][...] = value

    full = lambda shape: pl.BlockSpec(shape, lambda i, *_: (0,) * len(shape))
    return pl.pallas_call(
        body,
        grid_spec=pltpu.PrefetchScalarGridSpec(
            num_scalar_prefetch=1,
            grid=(1,),
            in_specs=[full(wholes[0].shape)] * len(wholes)
            + [full(shape)] * len(pieces)
            + [ANYWHERE] * len(waited),
            out_specs=[full(shape)] * size,
        ),
        out_shape=[jax.ShapeDtypeStruct(shape, jnp.float32)] * size,
        compiler_params=PARAMS,
        cost_estimate=SMALL,
        name="total",
    )(place, *wholes, *pieces, *waited)


def send_on(axis, parts):
    size = len(parts)
    return [parts[0]] + [
        lax.ppermute(parts[d], axis, [(s, (s + d) % size) for s in range(size)]) for d in range(1, size)
    ]


def join(early, late):
    def body(*refs):
        out = refs[-1]
        for srcs, low, high in ((refs[:NY], 0, EARLY), (refs[NY:-1], EARLY, EARLY + 2 * LATE)):
            value = srcs[0][...]
            for src in srcs[1:]:
                value = value + src[...]
            out[:, low:high] = value

    return pl.pallas_call(
        body,
        out_shape=jax.ShapeDtypeStruct((NZ * 2, EARLY + 2 * LATE, BS), jnp.float32),
        compiler_params=PARAMS,
        cost_estimate=SMALL,
        name="join",
    )(*early, *late)


def finish(parts, scale):
    count = parts.shape[1]

    def body(src, out):
        lane = lax.broadcasted_iota(jnp.int32, (OWNERS * LATE, BS), 1)
        for w in range(count):
            value = src[0, w]
            for s in range(1, NZ):
                value = value + src[s, w]
            value = value * scale
            packed = value[EARLY + LATE:]
            stacked = jnp.concatenate(
                [packed if q == 0 else pltpu.roll(packed, BS - q * EARLY, 1) for q in range(OWNERS)], axis=0
            )
            turned = jnp.concatenate([stacked] * (BS // (OWNERS * LATE)), axis=0).T
            rows = jnp.concatenate(
                [
                    jnp.where(lane[:EARLY] < EA, value[:EARLY], turned[:EARLY]),
                    value[EARLY:EARLY + LATE],
                ],
                axis=0,
            )
            result = jnp.zeros((EARLY + LATE, BS), jnp.float32)
            for o in range(OWNERS):
                at = o * (EARLY + LATE)
                for low, size, source in ((at, EARLY, o * EARLY), (at + EARLY, LATE, EA + o * LATE)):
                    by = (low - source) % BS
                    moved = pltpu.roll(rows, by, 1) if by else rows
                    result = jnp.where((lane >= low) & (lane < low + size), moved, result)
            out[w] = result

    return pl.pallas_call(
        body,
        out_shape=jax.ShapeDtypeStruct((count, EARLY + LATE, BS), jnp.float32),
        compiler_params=PARAMS,
        cost_estimate=SMALL,
        name="finish",
    )(parts)


def on_device(jac, obs_group, group_weight, pattern, pairs):
    total_obs = jac.shape[1] * NX
    core = lax.axis_index("c").astype(jnp.int32).reshape(1)
    listed = pairs.reshape(-1)
    choice = obs_group[0][None, :] == jnp.arange(group_weight.shape[0], dtype=jnp.int32)[:, None]
    root = jnp.sum(jnp.where(choice, group_weight[:, None], 0.0), axis=0)
    factors = pattern[0, 0].astype(jnp.float32)[:, None] * root[None, :]

    early = lax.all_to_all(relayout(jac, 0, EARLY), OBS_AXES, 0, 0, tiled=True)
    late = lax.all_to_all(relayout(jac, EARLY, LATE), OBS_AXES, 0, 0, tiled=True)

    give, keep, kept = early_tiles(early, factors, listed, core)
    kept = kept.reshape(2, NB, EA, -1)
    parts = total("x", [keep, swap_cores(give)], [])
    keep, *gives = late_tiles(late, kept, factors, listed, core, *parts)
    parts = total("y", send_on("x", parts), [])
    rest = total("x", [keep], [swap_cores(give) for give in gives], *parts)
    parts = send_on("y", parts)
    rest = total("y", send_on("x", rest), [])
    rest = send_on("y", rest)
    message = join(parts, rest).reshape(NZ, 2, EARLY + 2 * LATE, BS)
    owned = lax.all_to_all(message, "z", 0, 0, tiled=True)
    return finish(owned, 1.0 / math.sqrt(total_obs))


def solution(mesh):
    fine = Mesh(mesh.devices.reshape(NZ, NY, NC, NX), ("z", "y", "c", "x"))
    return jax.shard_map(
        on_device,
        mesh=fine,
        in_specs=(P(OBS_AXES, "x"), P("x", OBS_AXES), P(), P("x", OBS_AXES, None), P()),
        out_specs=P(OBS_AXES, "x", None),
        check_vma=False,
    )
```

time: 636 us -> 318 us (0.50)
  waiting for transfers between devices: 357 us -> 182 us
  local copies, waits for them, and re-layouts: 142 us -> 5.86 us
  matrix products: 99.5 us -> 0 us
  Pallas kernels: 0 us -> 71.2 us
  starting transfers between devices: 12.6 us -> 38 us
  blocking collectives: 0 us -> 19.5 us
  between operations: 13.5 us -> 0.25 us
  other arithmetic: 8.83 us -> 0.77 us
    reduce_scatter x2 -> x0, waiting for transfers between devices: 171 us -> none  [the longest x1 149 us: on_device(): owned = lax.psum_scatter(run(pairs), 'obs', scatter_dimension=0, tiled=True)]
    gather x32 -> x0, local copies, waits for them, and re-layouts: 134 us -> none  [the longest x8 61.6 us: group_tiles(): jblocks[first]]
    dot_general x8 -> x0, matrix products: 99.5 us -> none  [group_tiles(): jnp.einsum('pao,pbo->pab', jblocks[first], wblocks[second], precision=lax...]
    pallas_call x0 -> x10, Pallas kernels: none -> 71.2 us  [the longest x1 26 us: early_tiles(): pl.pallas_call(body, grid_spec=pltpu.PrefetchScalarGridSpec(num_scalar_pr...]
    all_to_all x1 -> x2, waiting for transfers between devices: 186 us -> 146 us  [the longest x1 136 us: on_device(): early = lax.all_to_all(relayout(jac, 0, EARLY), OBS_AXES, 0, 0, tiled=True)]
    ppermute x0 -> x17, waiting for transfers between devices: none -> 35.7 us  [the longest x12 29.8 us: send_on(): lax.ppermute(parts[d], axis, [(s, (s + d) % size) for s in range(size)])]
    ppermute x0 -> x17, starting transfers between devices: none -> 19.8 us  [the longest x12 18.6 us: send_on(): lax.ppermute(parts[d], axis, [(s, (s + d) % size) for s in range(size)])]
    all_to_all x0 -> x1, blocking collectives: none -> 19.5 us  [on_device(): owned = lax.all_to_all(message, 'z', 0, 0, tiled=True)]
  transfers between devices with their start and end apart: 3 -> 19, of which waited for: 3 -> 9; matrix products, arithmetic and copies ran while one was open for 0% -> 1% of each run, Pallas kernels for 0% -> 18%
where the time goes in v2:
time: 318 us; the launch traced here: 317 us
  waiting for transfers between devices  182 us (57%)
  Pallas kernels  71.2 us (22%)
  starting transfers between devices  38 us (12%)
  blocking collectives  19.5 us (6%)
  local copies, waits for them, and re-layouts  5.86 us (2%)
    all_to_all x1, waiting for transfers between devices, on_device(): early = lax.all_to_all(relayout(jac, 0, EARLY), OBS_AXES, 0, 0, tiled=True)  136 us
    ppermute x12, waiting for transfers between devices, send_on(): lax.ppermute(parts[d], axis, [(s, (s + d) % size) for s in range(size)])  29.8 us
    pallas_call x1, Pallas kernels, early_tiles(): pl.pallas_call(body, grid_spec=pltpu.PrefetchScalarGridSpec(num_scalar_pr...  26 us
    all_to_all x1, blocking collectives, on_device(): owned = lax.all_to_all(message, 'z', 0, 0, tiled=True)  19.5 us
    ppermute x12, starting transfers between devices, send_on(): lax.ppermute(parts[d], axis, [(s, (s + d) % size) for s in range(size)])  18.6 us
    pallas_call x1, Pallas kernels, late_tiles(): pl.pallas_call(body, grid_spec=pltpu.PrefetchScalarGridSpec(num_scalar_pr...  17.5 us
    pallas_call x4, Pallas kernels, total(): pl.pallas_call(body, grid_spec=pltpu.PrefetchScalarGridSpec(num_scalar_pr...  14.1 us
    all_to_all x1, starting transfers between devices, on_device(): early = lax.all_to_all(relayout(jac, 0, EARLY), OBS_AXES, 0, 0, tiled=True)  12.3 us
  transfers between devices with their start and end apart: 19, of which 9 were waited for; matrix products, arithmetic and copies ran while one was open for 1% of the time, Pallas kernels for 18%

profile of v2, /device:TPU:6, one launch (start us, length us, event | category | flops | bytes accessed | tf_op | source)
XLA Modules:
  0.0 317.2 jit_solution(10467902136100447096)
XLA Ops:
  0.0 6.3 %relayout.2 = f32[64,24,1024]{2,1,0:T(8,128)} custom-call(f32[32,65536]{1,0:T(8,128)} %src.3), custom_call_target="tpu_custom_call" | custom-call | flops 1 | bytes 1 | tf_op jit(solution)/shard_map/relayout/pallas_call | solution.py:41
  6.3 12.3 %all-to-all-start = ((f32[64,24,1024]{2,1,0:T(8,128)}), f32[64,24,1024]{2,1,0:T(8,128)}, u32[]{:S(2)}, u32[]{:S(2)}) async-start(f32[64,24,1024]{2,1,0:T(8,128)} %relayout.2), calls=%async_computation | async-start | bytes 12582912 | tf_op jit(solution)/shard_map/all_to_all | solution.py:382
  18.7 3.4 %relayout.3 = f32[64,8,1024]{2,1,0:T(8,128)} custom-call(f32[32,65536]{1,0:T(8,128)} %src.3), custom_call_target="tpu_custom_call" | custom-call | flops 1 | bytes 1 | tf_op jit(solution)/shard_map/relayout/pallas_call | solution.py:41
  23.7 136.1 %all-to-all-done.src = f32[64,24,1024]{2,1,0:T(8,128)} async-done(((f32[64,24,1024]{2,1,0:T(8,128)}), f32[64,24,1024]{2,1,0:T(8,128)}, u32[]{:S(2)}, u32[]{:S(2)}) %all-to-all-start) | async-done | bytes 6291488 | tf_op jit(solution)/shard_map/all_to_all | solution.py:382
  159.8 5.9 %all-to-all-start.1 = ((f32[64,8,1024]{2,1,0:T(8,128)}), f32[64,8,1024]{2,1,0:T(8,128)}, u32[]{:S(2)}, u32[]{:S(2)}) async-start(f32[64,8,1024]{2,1,0:T(8,128)} %relayout.3), calls=%async_computation.1 | async-start | bytes 4194304 | tf_op jit(solution)/shard_map/all_to_all | solution.py:383
  165.7 26.0 %early_tiles.1 = (f32[4,4,16,24,128]{4,3,2,1,0:T(8,128)}, f32[4,4,16,24,128]{4,3,2,1,0:T(8,128)}, bf16[2,1536,1024]{2,1,0:T(8,128)(2,1)}) custom-call(s32[256]{0:T(256)} %reshape.30.pairs_ref, s32[1]{0:T(128)} %bitcast.2.core_ref, f32[16,1024]{1,0:T(8,128)} %broadcast_multiply_fusion.fac, f32[64,24,1024]{2,1,0:T(8,128)} %all-to-all-done.src), custom_call_target="tpu_custom_call" | custom-call | flops 99999997952 | bytes 18874368 | tf_op jit(solution)/shard_map/early_tiles/pallas_call | solution.py:147
  191.8 5.9 %collective-permute-done.refs_1_ = f32[4,4,16,24,128]{4,3,2,1,0:T(8,128)S(1)} collective-permute-done((f32[4,4,16,24,128]{4,3,2,1,0:T(8,128)}, f32[4,4,16,24,128]{4,3,2,1,0:T(8,128)S(1)}, u32[]{:S(2)}, u32[]{:S(2)}) %collective-permute-start) | collective-permute-done | bytes 3145760 | tf_op jit(solution)/shard_map/ppermute | solution.py:266
  199.4 4.9 %total.4 = (f32[4,16,24,128]{3,2,1,0:T(8,128)}, f32[4,16,24,128]{3,2,1,0:T(8,128)}, f32[4,16,24,128]{3,2,1,0:T(8,128)}, f32[4,16,24,128]{3,2,1,0:T(8,128)}) custom-call(s32[1]{0:T(128)} %bitcast.1.place_ref, f32[4,4,16,24,128]{4,3,2,1,0:T(8,128)} %get-tuple-element.29.refs_0_, f32[4,4,16,24,128]{4,3,2,1,0:T(8,128)} %copy-done), custom_call_target="tpu_custom_call" | custom-call | flops 1 | bytes 1 | tf_op jit(solution)/shard_map/total/pallas_call | solution.py:292
  204.7 2.4 collective-permute-start.2
  207.2 9.7 %all-to-all-done.1.src = f32[64,8,1024]{2,1,0:T(8,128)} async-done(((f32[64,8,1024]{2,1,0:T(8,128)}), f32[64,8,1024]{2,1,0:T(8,128)}, u32[]{:S(2)}, u32[]{:S(2)}) %all-to-all-start.1) | async-done | bytes 2097184 | tf_op jit(solution)/shard_map/all_to_all | solution.py:383
  216.9 17.5 %late_tiles.1 = (f32[4,4,16,16,128]{4,3,2,1,0:T(8,128)}, f32[4,16,16,128]{3,2,1,0:T(8,128)}, f32[4,16,16,128]{3,2,1,0:T(8,128)}, f32[4,16,16,128]{3,2,1,0:T(8,128)}, f32[4,16,16,128]{3,2,1,0:T(8,128)}) custom-call(s32[256]{0:T(256)} %reshape.30.pairs_ref, s32[1]{0:T(128)} %bitcast.2.core_ref, f32[64,8,1024]{2,1,0:T(8,128)} %all-to-all-done.1.src, ...), custom_call_target="tpu_custom_call" | custom-call | flops 99999997952 | bytes 12582912 | tf_op jit(solution)/shard_map/late_tiles/pallas_call | solution.py:242
  235.6 7.1 %collective-permute-done.3.refs_3_ = f32[4,16,24,128]{3,2,1,0:T(8,128)S(1)} collective-permute-done((f32[4,16,24,128]{3,2,1,0:T(8,128)}, f32[4,16,24,128]{3,2,1,0:T(8,128)S(1)}, u32[]{:S(2)}, u32[]{:S(2)}) %collective-permute-start.3) | collective-permute-done | bytes 786464 | tf_op jit(solution)/shard_map/ppermute | solution.py:312
  243.5 3.0 total.5
  247.5 3.8 %total.6 = (f32[4,16,16,128]{3,2,1,0:T(8,128)}, f32[4,16,16,128]{3,2,1,0:T(8,128)}, f32[4,16,16,128]{3,2,1,0:T(8,128)}, f32[4,16,16,128]{3,2,1,0:T(8,128)}) custom-call(s32[1]{0:T(128)} %bitcast.1.place_ref, f32[4,4,16,16,128]{4,3,2,1,0:T(8,128)} %get-tuple-element.40.refs_0_, f32[4,16,16,128]{3,2,1,0:T(8,128)} %copy-done.5, ...), custom_call_target="tpu_custom_call" | custom-call | flops 1 | bytes 1 | tf_op jit(solution)/shard_map/total/pallas_call | solution.py:292
  255.9 2.7 collective-permute-start.5
  258.6 7.6 %collective-permute-done.11.refs_1_ = f32[4,16,16,128]{3,2,1,0:T(8,128)S(1)} collective-permute-done((f32[4,16,16,128]{3,2,1,0:T(8,128)}, f32[4,16,16,128]{3,2,1,0:T(8,128)S(1)}, u32[]{:S(2)}, u32[]{:S(2)}) %collective-permute-start.11) | collective-permute-done | bytes 524320 | tf_op jit(solution)/shard_map/ppermute | solution.py:312
  266.2 2.7 collective-permute-start.6
  269.0 10.2 %collective-permute-done.13.refs_3_ = f32[4,16,16,128]{3,2,1,0:T(8,128)S(1)} collective-permute-done((f32[4,16,16,128]{3,2,1,0:T(8,128)}, f32[4,16,16,128]{3,2,1,0:T(8,128)S(1)}, u32[]{:S(2)}, u32[]{:S(2)}) %collective-permute-start.13) | collective-permute-done | bytes 524320 | tf_op jit(solution)/shard_map/ppermute | solution.py:312
  280.0 2.5 total.7
  284.0 2.6 collective-permute-start.15
  289.4 3.7 %collective-permute-done.15.refs_6_ = f32[16,16,128]{2,1,0:T(8,128)S(1)} collective-permute-done((f32[16,16,128]{2,1,0:T(8,128)}, f32[16,16,128]{2,1,0:T(8,128)S(1)}, u32[]{:S(2)}, u32[]{:S(2)}) %collective-permute-start.15) | collective-permute-done | bytes 131104 | tf_op jit(solution)/shard_map/ppermute | solution.py:312
  293.7 2.1 join.1
  295.9 19.5 %all_to_all.15.src = f32[8,2,40,128]{3,2,1,0:T(8,128)} all-to-all(f32[8,2,40,128]{3,2,1,0:T(8,128)} %bitcast.8), channel_id=1, replica_groups=mesh['z'=8,'y'=4,'c'=2,'x'=4] {'z'}, dimensions={0} | all-to-all | bytes 655360 | tf_op jit(solution)/shard_map/all_to_all | solution.py:395
  315.4 1.8 finish.1
  (74 shorter events, 17.3 us)
Async XLA Ops:
  6.3 153.5 %all-to-all-start = ((f32[64,24,1024]{2,1,0:T(8,128)}), f32[64,24,1024]{2,1,0:T(8,128)}, u32[]{:S(2)}, u32[]{:S(2)}) async-start(f32[64,24,1024]{2,1,0:T(8,128)} %relayout.2), calls=%async_computation | async-start | bytes 12582912 | tf_op jit(solution)/shard_map/all_to_all | solution.py:382
  159.8 57.1 %all-to-all-start.1 = ((f32[64,8,1024]{2,1,0:T(8,128)}), f32[64,8,1024]{2,1,0:T(8,128)}, u32[]{:S(2)}, u32[]{:S(2)}) async-start(f32[64,8,1024]{2,1,0:T(8,128)} %relayout.3), calls=%async_computation.1 | async-start | bytes 4194304 | tf_op jit(solution)/shard_map/all_to_all | solution.py:383
  191.7 6.0 %collective-permute-start = (f32[4,4,16,24,128]{4,3,2,1,0:T(8,128)}, f32[4,4,16,24,128]{4,3,2,1,0:T(8,128)S(1)}, u32[]{:S(2)}, u32[]{:S(2)}) collective-permute-start(f32[4,4,16,24,128]{4,3,2,1,0:T(8,128)} %get-tuple-element.30), channel_id=1, source_target_pairs={{0,4},{4,0},{1,5},{5,1},{2,6},{6,2},{3,7},{7,3},{8,12},{12,8},{9,1... | collective-permute-start | bytes 9437192 | tf_op jit(solution)/shard_map/ppermute | solution.py:266
  204.2 30.8 %collective-permute-start.1 = (f32[4,16,24,128]{3,2,1,0:T(8,128)}, f32[4,16,24,128]{3,2,1,0:T(8,128)S(1)}, u32[]{:S(2)}, u32[]{:S(2)}) collective-permute-start(f32[4,16,24,128]{3,2,1,0:T(8,128)} %get-tuple-element.32.refs_1_), channel_id=1, source_target_pairs={{0,1},{1,2},{2,3},{3,0},{4,5},{5,6},{6,7},{7,4},{8,9},{9,10},{10,1... | collective-permute-start | bytes 2359304 | tf_op jit(solution)/shard_map/ppermute | solution.py:312
  204.7 30.4 %collective-permute-start.2 = (f32[4,16,24,128]{3,2,1,0:T(8,128)}, f32[4,16,24,128]{3,2,1,0:T(8,128)S(1)}, u32[]{:S(2)}, u32[]{:S(2)}) collective-permute-start(f32[4,16,24,128]{3,2,1,0:T(8,128)} %get-tuple-element.33.refs_2_), channel_id=1, source_target_pairs={{0,2},{1,3},{2,0},{3,1},{4,6},{5,7},{6,4},{7,5},{8,10},{9,11},{10,... | collective-permute-start | bytes 2359304 | tf_op jit(solution)/shard_map/ppermute | solution.py:312
  207.1 35.5 %collective-permute-start.3 = (f32[4,16,24,128]{3,2,1,0:T(8,128)}, f32[4,16,24,128]{3,2,1,0:T(8,128)S(1)}, u32[]{:S(2)}, u32[]{:S(2)}) collective-permute-start(f32[4,16,24,128]{3,2,1,0:T(8,128)} %get-tuple-element.34.refs_3_), channel_id=1, source_target_pairs={{0,3},{1,0},{2,1},{3,2},{4,7},{5,4},{6,5},{7,6},{8,11},{9,8},{10,9... | collective-permute-start | bytes 2359304 | tf_op jit(solution)/shard_map/ppermute | solution.py:312
  234.4 12.0 %collective-permute-start.10 = (f32[4,16,16,128]{3,2,1,0:T(8,128)}, f32[4,16,16,128]{3,2,1,0:T(8,128)S(1)}, u32[]{:S(2)}, u32[]{:S(2)}) collective-permute-start(f32[4,16,16,128]{3,2,1,0:T(8,128)} %get-tuple-element.44), channel_id=1, source_target_pairs={{0,4},{4,0},{1,5},{5,1},{2,6},{6,2},{3,7},{7,3},{8,12},{12,8},{9,1... | collective-permute-start | bytes 1572872 | tf_op jit(solution)/shard_map/ppermute | solution.py:266
  234.5 12.0 %collective-permute-start.7 = (f32[4,16,16,128]{3,2,1,0:T(8,128)}, f32[4,16,16,128]{3,2,1,0:T(8,128)S(1)}, u32[]{:S(2)}, u32[]{:S(2)}) collective-permute-start(f32[4,16,16,128]{3,2,1,0:T(8,128)} %get-tuple-element.41), channel_id=1, source_target_pairs={{0,4},{4,0},{1,5},{5,1},{2,6},{6,2},{3,7},{7,3},{8,12},{12,8},{9,1... | collective-permute-start | bytes 1572872 | tf_op jit(solution)/shard_map/ppermute | solution.py:266
  235.0 11.5 %collective-permute-start.8 = (f32[4,16,16,128]{3,2,1,0:T(8,128)}, f32[4,16,16,128]{3,2,1,0:T(8,128)}, u32[]{:S(2)}, u32[]{:S(2)}) collective-permute-start(f32[4,16,16,128]{3,2,1,0:T(8,128)} %get-tuple-element.42), channel_id=1, source_target_pairs={{0,4},{4,0},{1,5},{5,1},{2,6},{6,2},{3,7},{7,3},{8,12},{12,8},{9,1... | collective-permute-start | bytes 1572872 | tf_op jit(solution)/shard_map/ppermute | solution.py:266
  235.1 11.4 %collective-permute-start.9 = (f32[4,16,16,128]{3,2,1,0:T(8,128)}, f32[4,16,16,128]{3,2,1,0:T(8,128)}, u32[]{:S(2)}, u32[]{:S(2)}) collective-permute-start(f32[4,16,16,128]{3,2,1,0:T(8,128)} %get-tuple-element.43), channel_id=1, source_target_pairs={{0,4},{4,0},{1,5},{5,1},{2,6},{6,2},{3,7},{7,3},{8,12},{12,8},{9,1... | collective-permute-start | bytes 1572872 | tf_op jit(solution)/shard_map/ppermute | solution.py:266
  246.5 8.0 %copy-start.11 = (f32[16,24,128]{2,1,0:T(8,128)S(1)}, f32[16,24,128]{2,1,0:T(8,128)}, u32[]{:S(2)}) copy-start(f32[16,24,128]{2,1,0:T(8,128)} %get-tuple-element.36.refs_6_) | copy-start | bytes 589828
  246.5 9.5 %copy-start.10 = (f32[16,24,128]{2,1,0:T(8,128)S(1)}, f32[16,24,128]{2,1,0:T(8,128)}, u32[]{:S(2)}) copy-start(f32[16,24,128]{2,1,0:T(8,128)} %get-tuple-element.37.refs_7_) | copy-start | bytes 589828
  246.5 19.8 %copy-start.9 = (f32[16,24,128]{2,1,0:T(8,128)S(1)}, f32[16,24,128]{2,1,0:T(8,128)}, u32[]{:S(2)}) copy-start(f32[16,24,128]{2,1,0:T(8,128)} %get-tuple-element.38.refs_8_) | copy-start | bytes 589828
  251.2 15.0 %collective-permute-start.11 = (f32[4,16,16,128]{3,2,1,0:T(8,128)}, f32[4,16,16,128]{3,2,1,0:T(8,128)S(1)}, u32[]{:S(2)}, u32[]{:S(2)}) collective-permute-start(f32[4,16,16,128]{3,2,1,0:T(8,128)} %get-tuple-element.46), channel_id=1, source_target_pairs={{0,1},{1,2},{2,3},{3,0},{4,5},{5,6},{6,7},{7,4},{8,9},{9,10},{10,1... | collective-permute-start | bytes 1572872 | tf_op jit(solution)/shard_map/ppermute | solution.py:312
  252.5 16.5 %collective-permute-start.12 = (f32[4,16,16,128]{3,2,1,0:T(8,128)}, f32[4,16,16,128]{3,2,1,0:T(8,128)S(1)}, u32[]{:S(2)}, u32[]{:S(2)}) collective-permute-start(f32[4,16,16,128]{3,2,1,0:T(8,128)} %get-tuple-element.47), channel_id=1, source_target_pairs={{0,2},{1,3},{2,0},{3,1},{4,6},{5,7},{6,4},{7,5},{8,10},{9,11},{10,... | collective-permute-start | bytes 1572872 | tf_op jit(solution)/shard_map/ppermute | solution.py:312
  254.2 25.0 %collective-permute-start.13 = (f32[4,16,16,128]{3,2,1,0:T(8,128)}, f32[4,16,16,128]{3,2,1,0:T(8,128)S(1)}, u32[]{:S(2)}, u32[]{:S(2)}) collective-permute-start(f32[4,16,16,128]{3,2,1,0:T(8,128)} %get-tuple-element.48), channel_id=1, source_target_pairs={{0,3},{1,0},{2,1},{3,2},{4,7},{5,4},{6,5},{7,6},{8,11},{9,8},{10,9... | collective-permute-start | bytes 1572872 | tf_op jit(solution)/shard_map/ppermute | solution.py:312
  254.4 32.2 %collective-permute-start.4 = (f32[16,24,128]{2,1,0:T(8,128)S(1)}, f32[16,24,128]{2,1,0:T(8,128)S(1)}, u32[]{:S(2)}, u32[]{:S(2)}) collective-permute-start(f32[16,24,128]{2,1,0:T(8,128)S(1)} %copy-done.11), channel_id=1, source_target_pairs={{0,8},{8,16},{16,24},{24,0},{1,9},{9,17},{17,25},{25,1},{2,10},{10... | collective-permute-start | bytes 589832 | tf_op jit(solution)/shard_map/ppermute | solution.py:312
  255.9 32.2 %collective-permute-start.5 = (f32[16,24,128]{2,1,0:T(8,128)S(1)}, f32[16,24,128]{2,1,0:T(8,128)S(1)}, u32[]{:S(2)}, u32[]{:S(2)}) collective-permute-start(f32[16,24,128]{2,1,0:T(8,128)S(1)} %copy-done.10), channel_id=1, source_target_pairs={{0,16},{8,24},{16,0},{24,8},{1,17},{9,25},{17,1},{25,9},{2,18},{10... | collective-permute-start | bytes 589832 | tf_op jit(solution)/shard_map/ppermute | solution.py:312
  266.2 13.0 %copy-start.6 = (f32[4,16,16,128]{3,2,1,0:T(8,128)}, f32[4,16,16,128]{3,2,1,0:T(8,128)S(1)}, u32[]{:S(2)}) copy-start(f32[4,16,16,128]{3,2,1,0:T(8,128)S(1)} %collective-permute-done.11.refs_1_) | copy-start | bytes 1572868
  266.2 21.9 %collective-permute-start.6 = (f32[16,24,128]{2,1,0:T(8,128)S(1)}, f32[16,24,128]{2,1,0:T(8,128)S(1)}, u32[]{:S(2)}, u32[]{:S(2)}) collective-permute-start(f32[16,24,128]{2,1,0:T(8,128)S(1)} %copy-done.9), channel_id=1, source_target_pairs={{0,24},{8,0},{16,8},{24,16},{1,25},{9,1},{17,9},{25,17},{2,26},{10... | collective-permute-start | bytes 589832 | tf_op jit(solution)/shard_map/ppermute | solution.py:312
  269.0 10.2 %copy-start.7 = (f32[4,16,16,128]{3,2,1,0:T(8,128)}, f32[4,16,16,128]{3,2,1,0:T(8,128)S(1)}, u32[]{:S(2)}) copy-start(f32[4,16,16,128]{3,2,1,0:T(8,128)S(1)} %collective-permute-done.12.refs_2_) | copy-start | bytes 1572868
  282.5 6.9 %collective-permute-start.14 = (f32[16,16,128]{2,1,0:T(8,128)}, f32[16,16,128]{2,1,0:T(8,128)S(1)}, u32[]{:S(2)}, u32[]{:S(2)}) collective-permute-start(f32[16,16,128]{2,1,0:T(8,128)} %get-tuple-element.50), channel_id=1, source_target_pairs={{0,8},{8,16},{16,24},{24,0},{1,9},{9,17},{17,25},{25,1},{2,10},{10... | collective-permute-start | bytes 393224 | tf_op jit(solution)/shard_map/ppermute | solution.py:312
  284.0 9.0 %collective-permute-start.15 = (f32[16,16,128]{2,1,0:T(8,128)}, f32[16,16,128]{2,1,0:T(8,128)S(1)}, u32[]{:S(2)}, u32[]{:S(2)}) collective-permute-start(f32[16,16,128]{2,1,0:T(8,128)} %get-tuple-element.51), channel_id=1, source_target_pairs={{0,16},{8,24},{16,0},{24,8},{1,17},{9,25},{17,1},{25,9},{2,18},{10... | collective-permute-start | bytes 393224 | tf_op jit(solution)/shard_map/ppermute | solution.py:312
  286.6 6.4 %collective-permute-start.16 = (f32[16,16,128]{2,1,0:T(8,128)}, f32[16,16,128]{2,1,0:T(8,128)S(1)}, u32[]{:S(2)}, u32[]{:S(2)}) collective-permute-start(f32[16,16,128]{2,1,0:T(8,128)} %get-tuple-element.52), channel_id=1, source_target_pairs={{0,24},{8,0},{16,8},{24,16},{1,25},{9,1},{17,9},{25,17},{2,26},{10... | collective-permute-start | bytes 393224 | tf_op jit(solution)/shard_map/ppermute | solution.py:312
  (17 other events, 57.7 us)

commit v3 on v2

--- a/solution.py
+++ b/solution.py
@@ -14,6 +14,7 @@
 OWNERS = 4
 EARLY, LATE = 24, 8
 EA, LA = OWNERS * EARLY, OWNERS * LATE
+PACKED = 2 * EARLY - 8
 VMEM_LIMIT = 60 * 1024 * 1024
 SMALL = pl.CostEstimate(flops=1, bytes_accessed=1, transcendentals=0)
 PARAMS = pltpu.CompilerParams(vmem_limit_bytes=VMEM_LIMIT)
@@ -59,14 +60,14 @@
     return top, (value - top.astype(jnp.float32)).astype(jnp.bfloat16)
 
 
-def each_pair(pairs_ref, mine, store):
+def each_owner(pairs_ref, mine, store):
     def one(s, carry):
-        z, y, w = s // (NY * 2), (s // 2) % NY, s % 2
-        k = ((z * NY + y) * NC + mine) * 2 + w
-        store(y, z * 2 + w, pairs_ref[2 * k], pairs_ref[2 * k + 1])
+        z, y = s // NY, s % NY
+        k = ((z * NY + y) * NC + mine) * 2
+        store(z, y, [(pairs_ref[2 * k + 2 * w], pairs_ref[2 * k + 2 * w + 1]) for w in range(2)])
         return carry
 
-    lax.fori_loop(0, NZ * NY * 2, one, 0, unroll=8)
+    lax.fori_loop(0, NZ * NY, one, 0, unroll=4)
 
 
 def early_tiles(received, factors, pairs, core):
@@ -122,20 +123,29 @@
 
         for n, (dst, who) in enumerate(((give, 1 - core_ref[0]), (keep, core_ref[0]))):
 
-            def store(y, at, i, j, n=n):
-                rows = pl.multiple_of(i * EA, EA)
-                block = j * EA // BS
-                skip = j * EA - block * BS
-                back = lax.rem(BS - skip, BS)
-                near = pl.ds(pl.multiple_of(block * BS, BS), BS)
-                far = pl.ds(pl.multiple_of(block * BS + BS, BS), BS)
+            def store(z, y, pairs, n=n):
+                tiles = []
+                for i, j in pairs:
+                    rows = pl.multiple_of(i * EA, EA)
+                    block = j * EA // BS
+                    skip = j * EA - block * BS
+                    back = lax.rem(BS - skip, BS)
+                    near = pl.ds(pl.multiple_of(block * BS, BS), BS)
+                    far = pl.ds(pl.multiple_of(block * BS + BS, BS), BS)
+                    tiles.append([])
+                    for x in range(NX):
+                        which = pl.ds(rows + x * EARLY, EARLY)
+                        low = pltpu.roll(prod[which, near], back, 1)
+                        high = pltpu.roll(prod[which, far], back, 1)
+                        tiles[-1].append(jnp.where(lane < BS - skip, low, high))
                 for x in range(NX):
-                    which = pl.ds(rows + x * EARLY, EARLY)
-                    low = pltpu.roll(prod[which, near], back, 1)
-                    high = pltpu.roll(prod[which, far], back, 1)
-                    out[n, x, y, at] = jnp.where(lane < BS - skip, low, high)
-
-            each_pair(pairs_ref, who, store)
+                    head, tail = tiles[0][x], tiles[1][x]
+                    last = tail[EARLY - 8:]
+                    gaps = [pltpu.roll(last, EA - LA * q, 1) for q in range(EARLY // 8)]
+                    out[n, x, y, z, 0:EARLY] = jnp.where(lane < EA, head, jnp.concatenate(gaps, axis=0))
+                    out[n, x, y, z, EARLY:PACKED] = tail[:EARLY - 8]
+
+            each_owner(pairs_ref, who, store)
             send = pltpu.make_async_copy(out.at[n], dst, sems.at[pieces + 1 + n])
             send.start()
             sends.append(send)
@@ -143,7 +153,7 @@
             send.wait()
         save.wait()
 
-    shape = (NX, NY, NZ * 2, EARLY, BS)
+    shape = (NX, NY, NZ, PACKED, BS)
     return pl.pallas_call(
         body,
         grid_spec=pltpu.PrefetchScalarGridSpec(
@@ -214,22 +224,23 @@
 
         for n, who in enumerate((1 - core_ref[0], core_ref[0])):
 
-            def store(y, at, i, j, n=n):
-                part = prod[pl.ds(pl.multiple_of(i * LA, LA), LA), pl.ds(pl.multiple_of(j * BS, BS), BS)]
-                flip = prod[pl.ds(pl.multiple_of(j * LA, LA), LA), pl.ds(pl.multiple_of(i * BS, BS), BS)]
-                turn = [flip[q * LATE:(q + 1) * LATE] for q in range(OWNERS)]
-                for far in (2, 1):
-                    by = far * EARLY
-                    for q in range(OWNERS):
-                        if q & far == 0:
-                            u, v = turn[q], turn[q | far]
-                            turn[q] = jnp.where(masks[far], u, pltpu.roll(v, by, 1))
-                            turn[q | far] = jnp.where(masks[far], pltpu.roll(u, BS - by, 1), v)
-                for x in range(NX):
-                    out[n, x, y, at, 0:LATE] = part[x * LATE:(x + 1) * LATE]
-                    out[n, x, y, at, LATE:2 * LATE] = turn[x]
-
-            each_pair(pairs_ref, who, store)
+            def store(z, y, pairs, n=n):
+                for w, (i, j) in enumerate(pairs):
+                    part = prod[pl.ds(pl.multiple_of(i * LA, LA), LA), pl.ds(pl.multiple_of(j * BS, BS), BS)]
+                    flip = prod[pl.ds(pl.multiple_of(j * LA, LA), LA), pl.ds(pl.multiple_of(i * BS, BS), BS)]
+                    turn = [flip[q * LATE:(q + 1) * LATE] for q in range(OWNERS)]
+                    for far in (2, 1):
+                        by = far * EARLY
+                        for q in range(OWNERS):
+                            if q & far == 0:
+                                u, v = turn[q], turn[q | far]
+                                turn[q] = jnp.where(masks[far], u, pltpu.roll(v, by, 1))
+                                turn[q | far] = jnp.where(masks[far], pltpu.roll(u, BS - by, 1), v)
+                    for x in range(NX):
+                        out[n, x, z, y, w, 0:LATE] = part[x * LATE:(x + 1) * LATE]
+                        out[n, x, z, y, w, LATE:2 * LATE] = turn[x]
+
+            each_owner(pairs_ref, who, store)
             for x in range(NX):
                 dst = keep.at[x] if n else gives[x]
                 sends.append(pltpu.make_async_copy(out.at[n, x], dst, sems.at[NB // 2 + n * NX + x]))
@@ -237,7 +248,7 @@
         for send in sends:
             send.wait()
 
-    shape = (NX, NY, NZ * 2, 2 * LATE, BS)
+    shape = (NX, NZ, NY, 2, 2 * LATE, BS)
     whole = lambda shape: pl.BlockSpec(shape, lambda i, *_: (0,) * len(shape))
     return pl.pallas_call(
         body,
@@ -288,16 +299,17 @@
                         value = value + piece_refs[s][...]
                     outs[d][...] = value
 
-    full = lambda shape: pl.BlockSpec(shape, lambda i, *_: (0,) * len(shape))
+    tail = (0,) * (len(shape) - 1)
+    cut = (shape[0] // 2,) + shape[1:]
+    full = pl.BlockSpec((size,) + cut, lambda i, *_: (0, i) + tail)
+    part = pl.BlockSpec(cut, lambda i, *_: (i,) + tail)
     return pl.pallas_call(
         body,
         grid_spec=pltpu.PrefetchScalarGridSpec(
             num_scalar_prefetch=1,
-            grid=(1,),
-            in_specs=[full(wholes[0].shape)] * len(wholes)
-            + [full(shape)] * len(pieces)
-            + [ANYWHERE] * len(waited),
-            out_specs=[full(shape)] * size,
+            grid=(2,),
+            in_specs=[full] * len(wholes) + [part] * len(pieces) + [ANYWHERE] * len(waited),
+            out_specs=[part] * size,
         ),
         out_shape=[jax.ShapeDtypeStruct(shape, jnp.float32)] * size,
         compiler_params=PARAMS,
@@ -313,43 +325,50 @@
     ]
 
 
-def join(early, late):
+def merge(terms, *waited):
     def body(*refs):
-        out = refs[-1]
-        for srcs, low, high in ((refs[:NY], 0, EARLY), (refs[NY:-1], EARLY, EARLY + 2 * LATE)):
-            value = srcs[0][...]
-            for src in srcs[1:]:
-                value = value + src[...]
-            out[:, low:high] = value
-
-    return pl.pallas_call(
-        body,
-        out_shape=jax.ShapeDtypeStruct((NZ * 2, EARLY + 2 * LATE, BS), jnp.float32),
+        value = refs[0][...]
+        for ref in refs[1:len(terms)]:
+            value = value + ref[...]
+        refs[-1][...] = value
+
+    vmem = pl.BlockSpec(memory_space=pltpu.VMEM)
+    return pl.pallas_call(
+        body,
+        in_specs=[vmem] * len(terms) + [ANYWHERE] * len(waited),
+        out_specs=vmem,
+        out_shape=jax.ShapeDtypeStruct(terms[0].shape, jnp.float32),
         compiler_params=PARAMS,
         cost_estimate=SMALL,
-        name="join",
-    )(*early, *late)
-
-
-def finish(parts, scale):
-    count = parts.shape[1]
-
-    def body(src, out):
+        name="merge",
+    )(*terms, *waited)
+
+
+def finish(early, late, scale):
+    count = late.shape[1]
+
+    def body(first, second, out):
         lane = lax.broadcasted_iota(jnp.int32, (OWNERS * LATE, BS), 1)
+        head = sum((first[s] for s in range(1, first.shape[0])), first[0]) * scale
         for w in range(count):
-            value = src[0, w]
-            for s in range(1, NZ):
-                value = value + src[s, w]
-            value = value * scale
-            packed = value[EARLY + LATE:]
+            rest = sum((second[s, w] for s in range(1, second.shape[0])), second[0, w]) * scale
+            if w == 0:
+                top = head[:EARLY]
+            else:
+                last = jnp.zeros((8, BS), jnp.float32)
+                for q in range(EARLY // 8):
+                    moved = pltpu.roll(head[8 * q:8 * q + 8], (LA * q - EA) % BS, 1)
+                    last = jnp.where(lane[:8] // LA == q, moved, last)
+                top = jnp.concatenate([head[EARLY:], last], axis=0)
+            packed = rest[LATE:]
             stacked = jnp.concatenate(
                 [packed if q == 0 else pltpu.roll(packed, BS - q * EARLY, 1) for q in range(OWNERS)], axis=0
             )
             turned = jnp.concatenate([stacked] * (BS // (OWNERS * LATE)), axis=0).T
             rows = jnp.concatenate(
                 [
-                    jnp.where(lane[:EARLY] < EA, value[:EARLY], turned[:EARLY]),
-                    value[EARLY:EARLY + LATE],
+                    jnp.where(lane[:EARLY] < EA, top, turned[:EARLY]),
+                    rest[:LATE],
                 ],
                 axis=0,
             )
@@ -368,7 +387,7 @@
         compiler_params=PARAMS,
         cost_estimate=SMALL,
         name="finish",
-    )(parts)
+    )(early, late)
 
 
 def on_device(jac, obs_group, group_weight, pattern, pairs):
@@ -388,12 +407,11 @@
     keep, *gives = late_tiles(late, kept, factors, listed, core, *parts)
     parts = total("y", send_on("x", parts), [])
     rest = total("x", [keep], [swap_cores(give) for give in gives], *parts)
-    parts = send_on("y", parts)
-    rest = total("y", send_on("x", rest), [])
-    rest = send_on("y", rest)
-    message = join(parts, rest).reshape(NZ, 2, EARLY + 2 * LATE, BS)
-    owned = lax.all_to_all(message, "z", 0, 0, tiled=True)
-    return finish(owned, 1.0 / math.sqrt(total_obs))
+    parts = merge(send_on("y", parts))
+    parts = lax.all_to_all(parts, "z", 0, 0, tiled=True)
+    rest = merge(send_on("x", rest), parts).reshape(NZ * NY, 2, 2 * LATE, BS)
+    rest = lax.all_to_all(rest, ("z", "y"), 0, 0, tiled=True)
+    return finish(parts, rest, 1.0 / math.sqrt(total_obs))
 
 
 def solution(mesh):

time: 318 us -> 307 us (0.965)
  waiting for transfers between devices: 182 us -> 158 us
  blocking collectives: 19.5 us -> 40.2 us
  starting transfers between devices: 38 us -> 31.4 us
    ppermute x12 -> x9, waiting for transfers between devices: 29.8 us -> 6.85 us  [send_on(): lax.ppermute(parts[d], axis, [(s, (s + d) % size) for s in range(size)])]
    all_to_all x1 -> x2, blocking collectives: 19.5 us -> 40.2 us  [the longest x1 23.9 us: on_device(): rest = lax.all_to_all(rest, ('z', 'y'), 0, 0, tiled=True)]
    ppermute x12 -> x9, starting transfers between devices: 18.6 us -> 11.8 us  [send_on(): lax.ppermute(parts[d], axis, [(s, (s + d) % size) for s in range(size)])]
    pallas_call x4 -> x3, Pallas kernels: 14.1 us -> 9.62 us  [total(): pl.pallas_call(body, grid_spec=pltpu.PrefetchScalarGridSpec(num_scalar_pr...]
  transfers between devices with their start and end apart: 19 -> 16, of which waited for: 9 -> 6; matrix products, arithmetic and copies ran while one was open for 1% -> 1% of each run, Pallas kernels for 18% -> 19%
where the time goes in v3:
time: 307 us
  waiting for transfers between devices  158 us (51%)
  Pallas kernels  69.9 us (23%)
  blocking collectives  40.2 us (13%)
  starting transfers between devices  31.4 us (10%)
  local copies, waits for them, and re-layouts  6.17 us (2%)
    all_to_all x1, waiting for transfers between devices, on_device(): early = lax.all_to_all(relayout(jac, 0, EARLY), OBS_AXES, 0, 0, tiled=True)  136 us
    pallas_call x1, Pallas kernels, early_tiles(): pl.pallas_call(body, grid_spec=pltpu.PrefetchScalarGridSpec(num_scalar_pr...  27.9 us
    all_to_all x1, blocking collectives, on_device(): rest = lax.all_to_all(rest, ('z', 'y'), 0, 0, tiled=True)  23.9 us
    pallas_call x1, Pallas kernels, late_tiles(): pl.pallas_call(body, grid_spec=pltpu.PrefetchScalarGridSpec(num_scalar_pr...  16.4 us
    all_to_all x1, blocking collectives, on_device(): parts = lax.all_to_all(parts, 'z', 0, 0, tiled=True)  16.3 us
    all_to_all x1, starting transfers between devices, on_device(): early = lax.all_to_all(relayout(jac, 0, EARLY), OBS_AXES, 0, 0, tiled=True)  12.3 us
    ppermute x9, starting transfers between devices, send_on(): lax.ppermute(parts[d], axis, [(s, (s + d) % size) for s in range(size)])  11.8 us
    all_to_all x1, waiting for transfers between devices, on_device(): lax.all_to_all(relayout(jac, EARLY, LATE), OBS_AXES, 0, 0, tiled=True)  9.85 us
  transfers between devices with their start and end apart: 16, of which 6 were waited for; matrix products, arithmetic and copies ran while one was open for 1% of the time, Pallas kernels for 19%

profile of v3, /device:TPU:6, one launch (start us, length us, event | category | flops | bytes accessed | tf_op | source)
XLA Modules:
  0.0 306.7 jit_solution(8417281363541777113)
XLA Ops:
  0.0 6.3 %relayout.2 = f32[64,24,1024]{2,1,0:T(8,128)} custom-call(f32[32,65536]{1,0:T(8,128)} %src.3), custom_call_target="tpu_custom_call" | custom-call | flops 1 | bytes 1 | tf_op jit(solution)/shard_map/relayout/pallas_call | solution.py:42
  6.3 12.3 %all-to-all-start = ((f32[64,24,1024]{2,1,0:T(8,128)}), f32[64,24,1024]{2,1,0:T(8,128)}, u32[]{:S(2)}, u32[]{:S(2)}) async-start(f32[64,24,1024]{2,1,0:T(8,128)} %relayout.2), calls=%async_computation | async-start | bytes 12582912 | tf_op jit(solution)/shard_map/all_to_all | solution.py:401
  18.7 3.3 %relayout.3 = f32[64,8,1024]{2,1,0:T(8,128)} custom-call(f32[32,65536]{1,0:T(8,128)} %src.3), custom_call_target="tpu_custom_call" | custom-call | flops 1 | bytes 1 | tf_op jit(solution)/shard_map/relayout/pallas_call | solution.py:42
  23.7 136.1 %all-to-all-done.src = f32[64,24,1024]{2,1,0:T(8,128)} async-done(((f32[64,24,1024]{2,1,0:T(8,128)}), f32[64,24,1024]{2,1,0:T(8,128)}, u32[]{:S(2)}, u32[]{:S(2)}) %all-to-all-start) | async-done | bytes 6291488 | tf_op jit(solution)/shard_map/all_to_all | solution.py:401
  159.8 5.9 %all-to-all-start.2 = ((f32[64,8,1024]{2,1,0:T(8,128)}), f32[64,8,1024]{2,1,0:T(8,128)}, u32[]{:S(2)}, u32[]{:S(2)}) async-start(f32[64,8,1024]{2,1,0:T(8,128)} %relayout.3), calls=%async_computation.2 | async-start | bytes 4194304 | tf_op jit(solution)/shard_map/all_to_all | solution.py:402
  165.7 27.9 %early_tiles.1 = (f32[4,4,8,40,128]{4,3,2,1,0:T(8,128)}, f32[4,4,8,40,128]{4,3,2,1,0:T(8,128)}, bf16[2,1536,1024]{2,1,0:T(8,128)(2,1)}) custom-call(s32[256]{0:T(256)} %reshape.29.pairs_ref, s32[1]{0:T(128)} %bitcast.2.core_ref, f32[16,1024]{1,0:T(8,128)} %broadcast_multiply_fusion.fac, f32[64,24,1024]{2,1,0:T(8,128)} %all-to-all-done.src), custom_call_target="tpu_custom_call" | custom-call | flops 99999997952 | bytes 18874368 | tf_op jit(solution)/shard_map/early_tiles/pallas_call | solution.py:157
  193.7 5.1 %collective-permute-done.refs_1_ = f32[4,4,8,40,128]{4,3,2,1,0:T(8,128)S(1)} collective-permute-done((f32[4,4,8,40,128]{4,3,2,1,0:T(8,128)}, f32[4,4,8,40,128]{4,3,2,1,0:T(8,128)S(1)}, u32[]{:S(2)}, u32[]{:S(2)}) %collective-permute-start) | collective-permute-done | bytes 2621472 | tf_op jit(solution)/shard_map/ppermute | solution.py:277
  200.4 3.7 %total.3 = (f32[4,8,40,128]{3,2,1,0:T(8,128)}, f32[4,8,40,128]{3,2,1,0:T(8,128)}, f32[4,8,40,128]{3,2,1,0:T(8,128)}, f32[4,8,40,128]{3,2,1,0:T(8,128)}) custom-call(s32[1]{0:T(128)} %bitcast.1.place_ref, f32[4,4,8,40,128]{4,3,2,1,0:T(8,128)} %get-tuple-element.25.refs_0_, f32[4,4,8,40,128]{4,3,2,1,0:T(8,128)} %copy-done), custom_call_target="tpu_custom_call" | custom-call | flops 1 | bytes 1 | tf_op jit(solution)/shard_map/total/pallas_call | solution.py:306
  204.6 2.4 collective-permute-start.2
  207.0 9.8 %all-to-all-done.2.src = f32[64,8,1024]{2,1,0:T(8,128)} async-done(((f32[64,8,1024]{2,1,0:T(8,128)}), f32[64,8,1024]{2,1,0:T(8,128)}, u32[]{:S(2)}, u32[]{:S(2)}) %all-to-all-start.2) | async-done | bytes 2097184 | tf_op jit(solution)/shard_map/all_to_all | solution.py:402
  216.9 16.4 %late_tiles.1 = (f32[4,8,4,2,16,128]{5,4,3,2,1,0:T(8,128)}, f32[8,4,2,16,128]{4,3,2,1,0:T(8,128)}, f32[8,4,2,16,128]{4,3,2,1,0:T(8,128)}, f32[8,4,2,16,128]{4,3,2,1,0:T(8,128)}, f32[8,4,2,16,128]{4,3,2,1,0:T(8,128)}) custom-call(s32[256]{0:T(256)} %reshape.29.pairs_ref, s32[1]{0:T(128)} %bitcast.2.core_ref, f32[64,8,1024]{2,1,0:T(8,128)} %all-to-all-done.2.src, ...), custom_call_target="tpu_custom_call" | custom-call | flops 99999997952 | bytes 12582912 | tf_op jit(solution)/shard_map/late_tiles/pallas_call | solution.py:253
  234.6 2.3 collective-permute-done.3.refs_3_
  237.7 2.6 total.4
  240.3 1.6 collective-permute-start.4
  243.1 3.3 %total.5 = (f32[8,4,2,16,128]{4,3,2,1,0:T(8,128)}, f32[8,4,2,16,128]{4,3,2,1,0:T(8,128)}, f32[8,4,2,16,128]{4,3,2,1,0:T(8,128)}, f32[8,4,2,16,128]{4,3,2,1,0:T(8,128)}) custom-call(s32[1]{0:T(128)} %bitcast.1.place_ref, f32[4,8,4,2,16,128]{5,4,3,2,1,0:T(8,128)} %get-tuple-element.36.refs_0_, f32[8,4,2,16,128]{4,3,2,1,0:T(8,128)} %copy-done.5, ...), custom_call_target="tpu_custom_call" | custom-call | flops 1 | bytes 1 | tf_op jit(solution)/shard_map/total/pallas_call | solution.py:306
  247.6 1.8 collective-permute-start.12
  249.6 2.7 collective-permute-start.5
  253.8 2.6 collective-permute-done.5.refs_2_
  256.4 1.9 collective-permute-done.6.refs_3_
  259.0 1.8 merge.2
  260.8 16.3 %all_to_all.20.refs_4_.first = f32[8,40,128]{2,1,0:T(8,128)} all-to-all(f32[8,40,128]{2,1,0:T(8,128)} %merge.2), channel_id=1, replica_groups=mesh['z'=8,'y'=4,'c'=2,'x'=4] {'z'}, dimensions={0} | all-to-all | bytes 327680 | tf_op jit(solution)/shard_map/all_to_all | solution.py:411
  278.3 2.4 merge.3
  280.7 23.9 %all_to_all.21.second = f32[32,2,16,128]{3,2,1,0:T(8,128)} all-to-all(f32[32,2,16,128]{3,2,1,0:T(8,128)} %bitcast.8), channel_id=1, replica_groups=mesh['z'=8,'y'=4,'c'=2,'x'=4] {'z','y'}, dimensions={0} | all-to-all | bytes 1048576 | tf_op jit(solution)/shard_map/all_to_all | solution.py:413
  304.6 2.0 finish.1
  (63 shorter events, 11.7 us)
Async XLA Ops:
  6.3 153.5 %all-to-all-start = ((f32[64,24,1024]{2,1,0:T(8,128)}), f32[64,24,1024]{2,1,0:T(8,128)}, u32[]{:S(2)}, u32[]{:S(2)}) async-start(f32[64,24,1024]{2,1,0:T(8,128)} %relayout.2), calls=%async_computation | async-start | bytes 12582912 | tf_op jit(solution)/shard_map/all_to_all | solution.py:401
  18.6 3.4 %copy-start.16 = (s32[128,2]{0,1:T(2,128)S(1)}, s32[128,2]{0,1:T(2,128)}, u32[]{:S(2)}) copy-start(s32[128,2]{0,1:T(2,128)} %param.9) | copy-start | bytes 3076
  18.6 4.2 %copy-start.15 = (s32[1,1024]{1,0:T(1,128)S(1)}, s32[1,1024]{1,0:T(1,128)}, u32[]{:S(2)}) copy-start(s32[1,1024]{1,0:T(1,128)} %param.6) | copy-start | bytes 12292
  18.7 4.2 %copy-start.17 = (f32[16]{0:T(128)S(1)}, f32[16]{0:T(128)}, u32[]{:S(2)}) copy-start(f32[16]{0:T(128)} %param.7) | copy-start | bytes 196
  18.7 4.3 %copy-start.18 = (s32[1,1,16]{2,1,0:T(1,128)S(1)}, s32[1,1,16]{2,1,0:T(1,128)}, u32[]{:S(2)}) copy-start(s32[1,1,16]{2,1,0:T(1,128)} %param.8) | copy-start | bytes 196
  159.8 57.1 %all-to-all-start.2 = ((f32[64,8,1024]{2,1,0:T(8,128)}), f32[64,8,1024]{2,1,0:T(8,128)}, u32[]{:S(2)}, u32[]{:S(2)}) async-start(f32[64,8,1024]{2,1,0:T(8,128)} %relayout.3), calls=%async_computation.2 | async-start | bytes 4194304 | tf_op jit(solution)/shard_map/all_to_all | solution.py:402
  193.6 5.2 %collective-permute-start = (f32[4,4,8,40,128]{4,3,2,1,0:T(8,128)}, f32[4,4,8,40,128]{4,3,2,1,0:T(8,128)S(1)}, u32[]{:S(2)}, u32[]{:S(2)}) collective-permute-start(f32[4,4,8,40,128]{4,3,2,1,0:T(8,128)} %get-tuple-element.26), channel_id=1, source_target_pairs={{0,4},{4,0},{1,5},{5,1},{2,6},{6,2},{3,7},{7,3},{8,12},{12,8},{9,1... | collective-permute-start | bytes 7864328 | tf_op jit(solution)/shard_map/ppermute | solution.py:277
  204.1 29.9 %collective-permute-start.1 = (f32[4,8,40,128]{3,2,1,0:T(8,128)}, f32[4,8,40,128]{3,2,1,0:T(8,128)S(1)}, u32[]{:S(2)}, u32[]{:S(2)}) collective-permute-start(f32[4,8,40,128]{3,2,1,0:T(8,128)} %get-tuple-element.28.refs_1_), channel_id=1, source_target_pairs={{0,1},{1,2},{2,3},{3,0},{4,5},{5,6},{6,7},{7,4},{8,9},{9,10},{10,1... | collective-permute-start | bytes 1966088 | tf_op jit(solution)/shard_map/ppermute | solution.py:324
  204.6 29.5 %collective-permute-start.2 = (f32[4,8,40,128]{3,2,1,0:T(8,128)}, f32[4,8,40,128]{3,2,1,0:T(8,128)S(1)}, u32[]{:S(2)}, u32[]{:S(2)}) collective-permute-start(f32[4,8,40,128]{3,2,1,0:T(8,128)} %get-tuple-element.29.refs_2_), channel_id=1, source_target_pairs={{0,2},{1,3},{2,0},{3,1},{4,6},{5,7},{6,4},{7,5},{8,10},{9,11},{10,... | collective-permute-start | bytes 1966088 | tf_op jit(solution)/shard_map/ppermute | solution.py:324
  207.0 29.9 %collective-permute-start.3 = (f32[4,8,40,128]{3,2,1,0:T(8,128)}, f32[4,8,40,128]{3,2,1,0:T(8,128)S(1)}, u32[]{:S(2)}, u32[]{:S(2)}) collective-permute-start(f32[4,8,40,128]{3,2,1,0:T(8,128)} %get-tuple-element.30.refs_3_), channel_id=1, source_target_pairs={{0,3},{1,0},{2,1},{3,2},{4,7},{5,4},{6,5},{7,6},{8,11},{9,8},{10,9... | collective-permute-start | bytes 1966088 | tf_op jit(solution)/shard_map/ppermute | solution.py:324
  233.3 8.6 %collective-permute-start.10 = (f32[8,4,2,16,128]{4,3,2,1,0:T(8,128)}, f32[8,4,2,16,128]{4,3,2,1,0:T(8,128)S(1)}, u32[]{:S(2)}, u32[]{:S(2)}) collective-permute-start(f32[8,4,2,16,128]{4,3,2,1,0:T(8,128)} %get-tuple-element.40), channel_id=1, source_target_pairs={{0,4},{4,0},{1,5},{5,1},{2,6},{6,2},{3,7},{7,3},{8,12},{12,8},{9,1... | collective-permute-start | bytes 1572872 | tf_op jit(solution)/shard_map/ppermute | solution.py:277
  233.6 8.3 %collective-permute-start.7 = (f32[8,4,2,16,128]{4,3,2,1,0:T(8,128)}, f32[8,4,2,16,128]{4,3,2,1,0:T(8,128)S(1)}, u32[]{:S(2)}, u32[]{:S(2)}) collective-permute-start(f32[8,4,2,16,128]{4,3,2,1,0:T(8,128)} %get-tuple-element.37), channel_id=1, source_target_pairs={{0,4},{4,0},{1,5},{5,1},{2,6},{6,2},{3,7},{7,3},{8,12},{12,8},{9,1... | collective-permute-start | bytes 1572872 | tf_op jit(solution)/shard_map/ppermute | solution.py:277
  234.1 2.8 copy-start.1
  234.1 7.9 %collective-permute-start.8 = (f32[8,4,2,16,128]{4,3,2,1,0:T(8,128)}, f32[8,4,2,16,128]{4,3,2,1,0:T(8,128)S(1)}, u32[]{:S(2)}, u32[]{:S(2)}) collective-permute-start(f32[8,4,2,16,128]{4,3,2,1,0:T(8,128)} %get-tuple-element.38), channel_id=1, source_target_pairs={{0,4},{4,0},{1,5},{5,1},{2,6},{6,2},{3,7},{7,3},{8,12},{12,8},{9,1... | collective-permute-start | bytes 1572872 | tf_op jit(solution)/shard_map/ppermute | solution.py:277
  234.2 7.8 %collective-permute-start.9 = (f32[8,4,2,16,128]{4,3,2,1,0:T(8,128)}, f32[8,4,2,16,128]{4,3,2,1,0:T(8,128)}, u32[]{:S(2)}, u32[]{:S(2)}) collective-permute-start(f32[8,4,2,16,128]{4,3,2,1,0:T(8,128)} %get-tuple-element.39), channel_id=1, source_target_pairs={{0,4},{4,0},{1,5},{5,1},{2,6},{6,2},{3,7},{7,3},{8,12},{12,8},{9,1... | collective-permute-start | bytes 1572872 | tf_op jit(solution)/shard_map/ppermute | solution.py:277
  240.3 9.2 %copy-start.11 = (f32[8,40,128]{2,1,0:T(8,128)S(1)}, f32[8,40,128]{2,1,0:T(8,128)}, u32[]{:S(2)}) copy-start(f32[8,40,128]{2,1,0:T(8,128)} %get-tuple-element.33.refs_7_) | copy-start | bytes 491524
  240.3 11.9 %copy-start.10 = (f32[8,40,128]{2,1,0:T(8,128)S(1)}, f32[8,40,128]{2,1,0:T(8,128)}, u32[]{:S(2)}) copy-start(f32[8,40,128]{2,1,0:T(8,128)} %get-tuple-element.34.refs_8_) | copy-start | bytes 491524
  240.3 11.9 %collective-permute-start.4 = (f32[8,40,128]{2,1,0:T(8,128)}, f32[8,40,128]{2,1,0:T(8,128)S(1)}, u32[]{:S(2)}, u32[]{:S(2)}) collective-permute-start(f32[8,40,128]{2,1,0:T(8,128)} %get-tuple-element.32.refs_6_), channel_id=1, source_target_pairs={{0,8},{8,16},{16,24},{24,0},{1,9},{9,17},{17,25},{25,1},{2,10},{10... | collective-permute-start | bytes 491528 | tf_op jit(solution)/shard_map/ppermute | solution.py:324
  246.4 30.8 %collective-permute-start.11 = (f32[8,4,2,16,128]{4,3,2,1,0:T(8,128)}, f32[8,4,2,16,128]{4,3,2,1,0:T(8,128)S(1)}, u32[]{:S(2)}, u32[]{:S(2)}) collective-permute-start(f32[8,4,2,16,128]{4,3,2,1,0:T(8,128)} %get-tuple-element.42), channel_id=1, source_target_pairs={{0,1},{1,2},{2,3},{3,0},{4,5},{5,6},{6,7},{7,4},{8,9},{9,10},{10,1... | collective-permute-start | bytes 1572872 | tf_op jit(solution)/shard_map/ppermute | solution.py:324
  247.6 29.6 %collective-permute-start.12 = (f32[8,4,2,16,128]{4,3,2,1,0:T(8,128)}, f32[8,4,2,16,128]{4,3,2,1,0:T(8,128)S(1)}, u32[]{:S(2)}, u32[]{:S(2)}) collective-permute-start(f32[8,4,2,16,128]{4,3,2,1,0:T(8,128)} %get-tuple-element.43), channel_id=1, source_target_pairs={{0,2},{1,3},{2,0},{3,1},{4,6},{5,7},{6,4},{7,5},{8,10},{9,11},{10,... | collective-permute-start | bytes 1572872 | tf_op jit(solution)/shard_map/ppermute | solution.py:324
  249.4 27.8 %collective-permute-start.13 = (f32[8,4,2,16,128]{4,3,2,1,0:T(8,128)}, f32[8,4,2,16,128]{4,3,2,1,0:T(8,128)S(1)}, u32[]{:S(2)}, u32[]{:S(2)}) collective-permute-start(f32[8,4,2,16,128]{4,3,2,1,0:T(8,128)} %get-tuple-element.44), channel_id=1, source_target_pairs={{0,3},{1,0},{2,1},{3,2},{4,7},{5,4},{6,5},{7,6},{8,11},{9,8},{10,9... | collective-permute-start | bytes 1572872 | tf_op jit(solution)/shard_map/ppermute | solution.py:324
  249.6 6.8 %collective-permute-start.5 = (f32[8,40,128]{2,1,0:T(8,128)S(1)}, f32[8,40,128]{2,1,0:T(8,128)S(1)}, u32[]{:S(2)}, u32[]{:S(2)}) collective-permute-start(f32[8,40,128]{2,1,0:T(8,128)S(1)} %copy-done.11), channel_id=1, source_target_pairs={{0,16},{8,24},{16,0},{24,8},{1,17},{9,25},{17,1},{25,9},{2,18},{10... | collective-permute-start | bytes 491528 | tf_op jit(solution)/shard_map/ppermute | solution.py:324
  252.2 6.1 %copy-start.12 = (f32[8,40,128]{2,1,0:T(8,128)}, f32[8,40,128]{2,1,0:T(8,128)S(1)}, u32[]{:S(2)}) copy-start(f32[8,40,128]{2,1,0:T(8,128)S(1)} %collective-permute-done.4.refs_1_) | copy-start | bytes 491524
  252.2 6.1 %collective-permute-start.6 = (f32[8,40,128]{2,1,0:T(8,128)S(1)}, f32[8,40,128]{2,1,0:T(8,128)S(1)}, u32[]{:S(2)}, u32[]{:S(2)}) collective-permute-start(f32[8,40,128]{2,1,0:T(8,128)S(1)} %copy-done.10), channel_id=1, source_target_pairs={{0,24},{8,0},{16,8},{24,16},{1,25},{9,1},{17,9},{25,17},{2,26},{10... | collective-permute-start | bytes 491528 | tf_op jit(solution)/shard_map/ppermute | solution.py:324
  (11 other events, 13.5 us)

commit v4 on v3

--- a/solution.py
+++ b/solution.py
@@ -15,37 +15,46 @@
 EARLY, LATE = 24, 8
 EA, LA = OWNERS * EARLY, OWNERS * LATE
 PACKED = 2 * EARLY - 8
-VMEM_LIMIT = 60 * 1024 * 1024
+ANYWHERE = pl.BlockSpec(memory_space=pl.ANY)
 SMALL = pl.CostEstimate(flops=1, bytes_accessed=1, transcendentals=0)
-PARAMS = pltpu.CompilerParams(vmem_limit_bytes=VMEM_LIMIT)
-ANYWHERE = pl.BlockSpec(memory_space=pl.ANY)
+
+
+def room(mebibytes):
+    return pltpu.CompilerParams(vmem_limit_bytes=mebibytes * 2**20)
 
 
 def relayout(jac, start, rows):
     width = jac.shape[1] // PARTS
 
+    loads = 8
+    span = PARTS // loads
+
     def body(src, out, hold, sems):
-        loads, stores = [], []
-        for i in range(PARTS):
-            part = src.at[pl.ds(start, rows), pl.ds(i * width, width)]
-            loads.append(pltpu.make_async_copy(part, hold.at[i], sems.at[0, i]))
-            stores.append(pltpu.make_async_copy(hold.at[i], out.at[i], sems.at[1, i]))
-        for load in loads:
-            load.start()
-        for load, store in zip(loads, stores):
-            load.wait()
-            store.start()
+        copies = []
+        for n in range(loads):
+            lanes = pl.ds(n * span * width, span * width)
+            copies.append(pltpu.make_async_copy(src.at[pl.ds(start, rows), lanes], hold.at[:, lanes], sems.at[n]))
+            copies[-1].start()
+        stores = []
+        for n in range(loads):
+            copies[n].wait()
+            for i in range(n * span, (n + 1) * span):
+                lanes = pl.ds(i * width, width)
+                stores.append(pltpu.make_async_copy(hold.at[:, lanes], out.at[i], sems.at[loads + i]))
+                stores[-1].start()
         for store in stores:
             store.wait()
 
-    shape = (PARTS, rows, width)
     return pl.pallas_call(
         body,
         in_specs=[ANYWHERE],
         out_specs=ANYWHERE,
-        out_shape=jax.ShapeDtypeStruct(shape, jac.dtype),
-        scratch_shapes=[pltpu.VMEM(shape, jac.dtype), pltpu.SemaphoreType.DMA((2, PARTS))],
-        compiler_params=PARAMS,
+        out_shape=jax.ShapeDtypeStruct((PARTS, rows, width), jac.dtype),
+        scratch_shapes=[
+            pltpu.VMEM((rows, PARTS * width), jac.dtype),
+            pltpu.SemaphoreType.DMA((loads + PARTS,)),
+        ],
+        compiler_params=room(60),
         cost_estimate=SMALL,
         name="relayout",
     )(jac)
@@ -86,13 +95,28 @@
         ]
         for load in loads:
             load.start()
-        prod[:, total:] = jnp.zeros((total, BS), jnp.float32)
+        lane = lax.broadcasted_iota(jnp.int32, (tall, BS), 1)
 
         def convert(i, carry):
             value = arrived[pl.ds(i * OWNERS, OWNERS)].reshape(EA, width) * fac[pl.ds(i, 1), :]
             rows = pl.ds(pl.multiple_of(i * EA, EA), EA)
             halves[0, rows, :], halves[1, rows, :] = split(value)
             return carry
+
+        def place(rows, start, value):
+            stop = start + value.shape[1]
+            for j in range(start // EA, -(-stop // EA)):
+                low, high = max(j * EA, start), min((j + 1) * EA, stop)
+                by = (start - j * EA) % BS
+                moved = None
+                for t in range((low - start) // BS, (high - start - 1) // BS + 1):
+                    part = value[:, t * BS:(t + 1) * BS]
+                    part = pltpu.roll(part, by, 1) if by else part
+                    moved = part if moved is None else jnp.where(lane < start + t * BS - j * EA, moved, part)
+                block = slice(j * BS, (j + 1) * BS)
+                if low > j * EA:
+                    moved = jnp.where(lane < low - j * EA, prod[rows, block], moved)
+                prod[rows, block] = moved
 
         ready = 0
         for g in range(total // tall):
@@ -102,23 +126,25 @@
                 ready += 1
             cols = slice(g * tall, (g + 1) * tall)
 
-            def row(a, carry, cols=cols):
+            def row(a, carry, cols=cols, g=g):
                 rows = pl.ds(pl.multiple_of(a * tall, tall), tall)
                 ah, al = halves[0, rows, :], halves[1, rows, :]
                 bh, bl = halves[0, cols, :], halves[1, cols, :]
-                prod[rows, cols] = dot(ah, bh) + (dot(ah, bl) + dot(al, bh))
+                place(rows, g * tall, dot(ah, bh) + (dot(ah, bl) + dot(al, bh)))
                 return carry
 
             lax.fori_loop(0, g + 1, row, 0)
-            if g:
-                rows, cols = slice(g * tall, g * tall + 64), slice(g * tall - BS, g * tall)
+            if g * tall % EA:
+                rows = slice(g * tall, g * tall + 64)
+                cols = slice(g * tall // EA * EA, g * tall)
                 ah, al = halves[0, rows, :], halves[1, rows, :]
                 bh, bl = halves[0, cols, :], halves[1, cols, :]
-                prod[rows, cols] = dot(ah, bh) + (dot(ah, bl) + dot(al, bh))
+                value = dot(ah, bh) + (dot(ah, bl) + dot(al, bh))
+                at = g * tall // EA * BS
+                prod[rows, at:at + value.shape[1]] = value
 
         save = pltpu.make_async_copy(halves, kept, sems.at[pieces])
         save.start()
-        lane = lax.broadcasted_iota(jnp.int32, (EARLY, BS), 1)
         sends = []
 
         for n, (dst, who) in enumerate(((give, 1 - core_ref[0]), (keep, core_ref[0]))):
@@ -127,22 +153,13 @@
                 tiles = []
                 for i, j in pairs:
                     rows = pl.multiple_of(i * EA, EA)
-                    block = j * EA // BS
-                    skip = j * EA - block * BS
-                    back = lax.rem(BS - skip, BS)
-                    near = pl.ds(pl.multiple_of(block * BS, BS), BS)
-                    far = pl.ds(pl.multiple_of(block * BS + BS, BS), BS)
-                    tiles.append([])
-                    for x in range(NX):
-                        which = pl.ds(rows + x * EARLY, EARLY)
-                        low = pltpu.roll(prod[which, near], back, 1)
-                        high = pltpu.roll(prod[which, far], back, 1)
-                        tiles[-1].append(jnp.where(lane < BS - skip, low, high))
+                    cols = pl.ds(pl.multiple_of(j * BS, BS), BS)
+                    tiles.append([prod[pl.ds(rows + x * EARLY, EARLY), cols] for x in range(NX)])
                 for x in range(NX):
                     head, tail = tiles[0][x], tiles[1][x]
                     last = tail[EARLY - 8:]
                     gaps = [pltpu.roll(last, EA - LA * q, 1) for q in range(EARLY // 8)]
-                    out[n, x, y, z, 0:EARLY] = jnp.where(lane < EA, head, jnp.concatenate(gaps, axis=0))
+                    out[n, x, y, z, 0:EARLY] = jnp.where(lane[:EARLY] < EA, head, jnp.concatenate(gaps, axis=0))
                     out[n, x, y, z, EARLY:PACKED] = tail[:EARLY - 8]
 
             each_owner(pairs_ref, who, store)
@@ -164,14 +181,14 @@
             scratch_shapes=[
                 pltpu.VMEM(received.shape, jnp.float32),
                 pltpu.VMEM((2, total, width), jnp.bfloat16),
-                pltpu.VMEM((total, total + BS), jnp.float32),
+                pltpu.VMEM((total, NB * BS), jnp.float32),
                 pltpu.VMEM((2,) + shape, jnp.float32),
                 pltpu.SemaphoreType.DMA((pieces + 3,)),
             ],
         ),
         out_shape=[jax.ShapeDtypeStruct(shape, jnp.float32)] * 2
         + [jax.ShapeDtypeStruct((2, total, width), jnp.bfloat16)],
-        compiler_params=PARAMS,
+        compiler_params=room(58),
         cost_estimate=pl.CostEstimate(flops=10**11, bytes_accessed=18 * 2**20, transcendentals=0),
         name="early_tiles",
     )(pairs, core, factors, received)
@@ -267,7 +284,7 @@
         ),
         out_shape=[jax.ShapeDtypeStruct(shape, jnp.float32)]
         + [jax.ShapeDtypeStruct(shape[1:], jnp.float32)] * NX,
-        compiler_params=PARAMS,
+        compiler_params=room(58),
         cost_estimate=pl.CostEstimate(flops=10**11, bytes_accessed=12 * 2**20, transcendentals=0),
         name="late_tiles",
     )(pairs, core, received, factors, kept, *waited)
@@ -312,7 +329,7 @@
             out_specs=[part] * size,
         ),
         out_shape=[jax.ShapeDtypeStruct(shape, jnp.float32)] * size,
-        compiler_params=PARAMS,
+        compiler_params=room(16),
         cost_estimate=SMALL,
         name="total",
     )(place, *wholes, *pieces, *waited)
@@ -338,7 +355,7 @@
         in_specs=[vmem] * len(terms) + [ANYWHERE] * len(waited),
         out_specs=vmem,
         out_shape=jax.ShapeDtypeStruct(terms[0].shape, jnp.float32),
-        compiler_params=PARAMS,
+        compiler_params=room(16),
         cost_estimate=SMALL,
         name="merge",
     )(*terms, *waited)
@@ -384,7 +401,7 @@
     return pl.pallas_call(
         body,
         out_shape=jax.ShapeDtypeStruct((count, EARLY + LATE, BS), jnp.float32),
-        compiler_params=PARAMS,
+        compiler_params=room(16),
         cost_estimate=SMALL,
         name="finish",
     )(early, late)

time: 307 us -> 293 us (0.954)
  Pallas kernels: 69.9 us -> 55.8 us
  waiting for transfers between devices: 158 us -> 165 us
  blocking collectives: 40.2 us -> 36.8 us
    all_to_all x1, waiting for transfers between devices: 9.85 us -> 14.5 us  [on_device(): lax.all_to_all(relayout(jac, EARLY, LATE), OBS_AXES, 0, 0, tiled=True)]
    all_to_all x1, blocking collectives: 16.3 us -> 11.8 us  [on_device(): parts = lax.all_to_all(parts, 'z', 0, 0, tiled=True)]
    pallas_call x3, Pallas kernels: 9.62 us -> 5.19 us  [total(): pl.pallas_call(body, grid_spec=pltpu.PrefetchScalarGridSpec(num_scalar_pr...]
    pallas_call x2, Pallas kernels: 4.27 us -> 0.13 us  [merge(): pl.pallas_call(body, in_specs=[vmem] * len(terms) + [ANYWHERE] * len(wait...]
    pallas_call x1, Pallas kernels: 27.9 us -> 24.1 us  [early_tiles(): pl.pallas_call(body, grid_spec=pltpu.PrefetchScalarGridSpec(num_scalar_pr...]
  transfers between devices with their start and end apart: 16 -> 16, of which waited for: 6 -> 7; matrix products, arithmetic and copies ran while one was open for 1% -> 1% of each run, Pallas kernels for 19% -> 17%
where the time goes in v4:
time: 293 us
  waiting for transfers between devices  165 us (56%)
  Pallas kernels  55.8 us (19%)
  blocking collectives  36.8 us (13%)
  starting transfers between devices  31 us (11%)
  local copies, waits for them, and re-layouts  3.44 us (1%)
    all_to_all x1, waiting for transfers between devices, on_device(): early = lax.all_to_all(relayout(jac, 0, EARLY), OBS_AXES, 0, 0, tiled=True)  136 us
    all_to_all x1, blocking collectives, on_device(): rest = lax.all_to_all(rest, ('z', 'y'), 0, 0, tiled=True)  25 us
    pallas_call x1, Pallas kernels, early_tiles(): pl.pallas_call(body, grid_spec=pltpu.PrefetchScalarGridSpec(num_scalar_pr...  24.1 us
    pallas_call x1, Pallas kernels, late_tiles(): pl.pallas_call(body, grid_spec=pltpu.PrefetchScalarGridSpec(num_scalar_pr...  16.5 us
    all_to_all x1, waiting for transfers between devices, on_device(): lax.all_to_all(relayout(jac, EARLY, LATE), OBS_AXES, 0, 0, tiled=True)  14.5 us
    all_to_all x1, starting transfers between devices, on_device(): early = lax.all_to_all(relayout(jac, 0, EARLY), OBS_AXES, 0, 0, tiled=True)  12.3 us
    all_to_all x1, blocking collectives, on_device(): parts = lax.all_to_all(parts, 'z', 0, 0, tiled=True)  11.8 us
    ppermute x9, starting transfers between devices, send_on(): lax.ppermute(parts[d], axis, [(s, (s + d) % size) for s in range(size)])  11.6 us
  transfers between devices with their start and end apart: 16, of which 7 were waited for; matrix products, arithmetic and copies ran while one was open for 1% of the time, Pallas kernels for 17%

profile of v4, /device:TPU:6, one launch (start us, length us, event | category | flops | bytes accessed | tf_op | source)
XLA Modules:
  0.0 292.6 jit_solution(3137074139400735023)
XLA Ops:
  0.0 6.0 %relayout.2 = f32[64,24,1024]{2,1,0:T(8,128)} custom-call(f32[32,65536]{1,0:T(8,128)} %src.3), custom_call_target="tpu_custom_call" | custom-call | flops 1 | bytes 1 | tf_op jit(solution)/shard_map/relayout/pallas_call | solution.py:48
  6.0 12.3 %all-to-all-start = ((f32[64,24,1024]{2,1,0:T(8,128)}), f32[64,24,1024]{2,1,0:T(8,128)}, u32[]{:S(2)}, u32[]{:S(2)}) async-start(f32[64,24,1024]{2,1,0:T(8,128)} %relayout.2), calls=%async_computation | async-start | bytes 12582912 | tf_op jit(solution)/shard_map/all_to_all | solution.py:418
  18.4 3.0 %relayout.3 = f32[64,8,1024]{2,1,0:T(8,128)} custom-call(f32[32,65536]{1,0:T(8,128)} %src.3), custom_call_target="tpu_custom_call" | custom-call | flops 1 | bytes 1 | tf_op jit(solution)/shard_map/relayout/pallas_call | solution.py:48
  23.0 136.5 %all-to-all-done.src = f32[64,24,1024]{2,1,0:T(8,128)} async-done(((f32[64,24,1024]{2,1,0:T(8,128)}), f32[64,24,1024]{2,1,0:T(8,128)}, u32[]{:S(2)}, u32[]{:S(2)}) %all-to-all-start) | async-done | bytes 6291488 | tf_op jit(solution)/shard_map/all_to_all | solution.py:418
  159.5 5.9 %all-to-all-start.2 = ((f32[64,8,1024]{2,1,0:T(8,128)}), f32[64,8,1024]{2,1,0:T(8,128)}, u32[]{:S(2)}, u32[]{:S(2)}) async-start(f32[64,8,1024]{2,1,0:T(8,128)} %relayout.3), calls=%async_computation.2 | async-start | bytes 4194304 | tf_op jit(solution)/shard_map/all_to_all | solution.py:419
  165.4 24.1 %early_tiles.1 = (f32[4,4,8,40,128]{4,3,2,1,0:T(8,128)}, f32[4,4,8,40,128]{4,3,2,1,0:T(8,128)}, bf16[2,1536,1024]{2,1,0:T(8,128)(2,1)}) custom-call(s32[256]{0:T(256)} %reshape.29.pairs_ref, s32[1]{0:T(128)} %bitcast.2.core_ref, f32[16,1024]{1,0:T(8,128)} %broadcast_multiply_fusion.fac, f32[64,24,1024]{2,1,0:T(8,128)} %all-to-all-done.src), custom_call_target="tpu_custom_call" | custom-call | flops 99999997952 | bytes 18874368 | tf_op jit(solution)/shard_map/early_tiles/pallas_call | solution.py:174
  189.6 5.1 %collective-permute-done.refs_1_ = f32[4,4,8,40,128]{4,3,2,1,0:T(8,128)S(1)} collective-permute-done((f32[4,4,8,40,128]{4,3,2,1,0:T(8,128)}, f32[4,4,8,40,128]{4,3,2,1,0:T(8,128)S(1)}, u32[]{:S(2)}, u32[]{:S(2)}) %collective-permute-start) | collective-permute-done | bytes 2621472 | tf_op jit(solution)/shard_map/ppermute | solution.py:294
  194.7 1.7 copy-done
  196.5 1.9 total.3
  199.7 2.4 collective-permute-start.2
  202.1 14.5 %all-to-all-done.2.src = f32[64,8,1024]{2,1,0:T(8,128)} async-done(((f32[64,8,1024]{2,1,0:T(8,128)}), f32[64,8,1024]{2,1,0:T(8,128)}, u32[]{:S(2)}, u32[]{:S(2)}) %all-to-all-start.2) | async-done | bytes 2097184 | tf_op jit(solution)/shard_map/all_to_all | solution.py:419
  216.6 16.5 %late_tiles.1 = (f32[4,8,4,2,16,128]{5,4,3,2,1,0:T(8,128)}, f32[8,4,2,16,128]{4,3,2,1,0:T(8,128)}, f32[8,4,2,16,128]{4,3,2,1,0:T(8,128)}, f32[8,4,2,16,128]{4,3,2,1,0:T(8,128)}, f32[8,4,2,16,128]{4,3,2,1,0:T(8,128)}) custom-call(s32[256]{0:T(256)} %reshape.29.pairs_ref, s32[1]{0:T(128)} %bitcast.2.core_ref, f32[64,8,1024]{2,1,0:T(8,128)} %all-to-all-done.2.src, ...), custom_call_target="tpu_custom_call" | custom-call | flops 99999997952 | bytes 12582912 | tf_op jit(solution)/shard_map/late_tiles/pallas_call | solution.py:270
  234.3 1.5 total.4
  235.8 1.5 collective-permute-start.4
  237.8 1.8 total.5
  240.1 2.4 collective-permute-start.12
  242.5 3.0 %collective-permute-start.5 = (f32[8,40,128]{2,1,0:T(8,128)S(1)}, f32[8,40,128]{2,1,0:T(8,128)S(1)}, u32[]{:S(2)}, u32[]{:S(2)}) collective-permute-start(f32[8,40,128]{2,1,0:T(8,128)S(1)} %get-tuple-element.33.refs_7_), channel_id=1, source_target_pairs={{0,16},{8,24},{16,0},{24,8},{1,17},{9,25},{17,1},{25,9},{2,18},{10... | collective-permute-start | bytes 491528 | tf_op jit(solution)/shard_map/ppermute | solution.py:341
  245.5 1.2 collective-permute-start.6
  246.7 3.0 %collective-permute-done.5.refs_2_ = f32[8,40,128]{2,1,0:T(8,128)S(1)} collective-permute-done((f32[8,40,128]{2,1,0:T(8,128)S(1)}, f32[8,40,128]{2,1,0:T(8,128)S(1)}, u32[]{:S(2)}, u32[]{:S(2)}) %collective-permute-start.5) | collective-permute-done | bytes 163872 | tf_op jit(solution)/shard_map/ppermute | solution.py:341
  249.7 3.6 %collective-permute-done.6.refs_3_ = f32[8,40,128]{2,1,0:T(8,128)S(1)} collective-permute-done((f32[8,40,128]{2,1,0:T(8,128)S(1)}, f32[8,40,128]{2,1,0:T(8,128)S(1)}, u32[]{:S(2)}, u32[]{:S(2)}) %collective-permute-start.6) | collective-permute-done | bytes 163872 | tf_op jit(solution)/shard_map/ppermute | solution.py:341
  253.3 11.8 %all_to_all.20.refs_4_.first = f32[8,40,128]{2,1,0:T(8,128)S(1)} all-to-all(f32[8,40,128]{2,1,0:T(8,128)S(1)} %merge.2), channel_id=1, replica_groups=mesh['z'=8,'y'=4,'c'=2,'x'=4] {'z'}, dimensions={0} | all-to-all | bytes 327680 | tf_op jit(solution)/shard_map/all_to_all | solution.py:428
  265.2 1.4 collective-permute-done.13.refs_3_
  266.7 25.0 %all_to_all.21.second = f32[32,2,16,128]{3,2,1,0:T(8,128)S(1)} all-to-all(f32[32,2,16,128]{3,2,1,0:T(8,128)S(1)} %bitcast.8), channel_id=1, replica_groups=mesh['z'=8,'y'=4,'c'=2,'x'=4] {'z','y'}, dimensions={0} | all-to-all | bytes 1048576 | tf_op jit(solution)/shard_map/all_to_all | solution.py:430
  291.7 0.9 finish.1
  (41 shorter events, 5.2 us)
Async XLA Ops:
  6.0 153.5 %all-to-all-start = ((f32[64,24,1024]{2,1,0:T(8,128)}), f32[64,24,1024]{2,1,0:T(8,128)}, u32[]{:S(2)}, u32[]{:S(2)}) async-start(f32[64,24,1024]{2,1,0:T(8,128)} %relayout.2), calls=%async_computation | async-start | bytes 12582912 | tf_op jit(solution)/shard_map/all_to_all | solution.py:418
  18.4 3.1 %copy-start.5 = (s32[128,2]{0,1:T(2,128)S(1)}, s32[128,2]{0,1:T(2,128)}, u32[]{:S(2)}) copy-start(s32[128,2]{0,1:T(2,128)} %param.9) | copy-start | bytes 3076
  18.4 3.9 %copy-start.4 = (s32[1,1024]{1,0:T(1,128)S(1)}, s32[1,1024]{1,0:T(1,128)}, u32[]{:S(2)}) copy-start(s32[1,1024]{1,0:T(1,128)} %param.6) | copy-start | bytes 12292
  18.4 3.9 %copy-start.6 = (f32[16]{0:T(128)S(1)}, f32[16]{0:T(128)}, u32[]{:S(2)}) copy-start(f32[16]{0:T(128)} %param.7) | copy-start | bytes 196
  18.4 3.9 %copy-start.7 = (s32[1,1,16]{2,1,0:T(1,128)S(1)}, s32[1,1,16]{2,1,0:T(1,128)}, u32[]{:S(2)}) copy-start(s32[1,1,16]{2,1,0:T(1,128)} %param.8) | copy-start | bytes 196
  159.5 57.1 %all-to-all-start.2 = ((f32[64,8,1024]{2,1,0:T(8,128)}), f32[64,8,1024]{2,1,0:T(8,128)}, u32[]{:S(2)}, u32[]{:S(2)}) async-start(f32[64,8,1024]{2,1,0:T(8,128)} %relayout.3), calls=%async_computation.2 | async-start | bytes 4194304 | tf_op jit(solution)/shard_map/all_to_all | solution.py:419
  189.5 5.2 %collective-permute-start = (f32[4,4,8,40,128]{4,3,2,1,0:T(8,128)}, f32[4,4,8,40,128]{4,3,2,1,0:T(8,128)S(1)}, u32[]{:S(2)}, u32[]{:S(2)}) collective-permute-start(f32[4,4,8,40,128]{4,3,2,1,0:T(8,128)} %get-tuple-element.26), channel_id=1, source_target_pairs={{0,4},{4,0},{1,5},{5,1},{2,6},{6,2},{3,7},{7,3},{8,12},{12,8},{9,1... | collective-permute-start | bytes 7864328 | tf_op jit(solution)/shard_map/ppermute | solution.py:294
  194.7 1.7 copy-start
  198.3 0.8 copy-start.2
  199.2 34.6 %collective-permute-start.1 = (f32[4,8,40,128]{3,2,1,0:T(8,128)}, f32[4,8,40,128]{3,2,1,0:T(8,128)S(1)}, u32[]{:S(2)}, u32[]{:S(2)}) collective-permute-start(f32[4,8,40,128]{3,2,1,0:T(8,128)} %get-tuple-element.28.refs_1_), channel_id=1, source_target_pairs={{0,1},{1,2},{2,3},{3,0},{4,5},{5,6},{6,7},{7,4},{8,9},{9,10},{10,1... | collective-permute-start | bytes 1966088 | tf_op jit(solution)/shard_map/ppermute | solution.py:341
  199.7 34.4 %collective-permute-start.2 = (f32[4,8,40,128]{3,2,1,0:T(8,128)}, f32[4,8,40,128]{3,2,1,0:T(8,128)}, u32[]{:S(2)}, u32[]{:S(2)}) collective-permute-start(f32[4,8,40,128]{3,2,1,0:T(8,128)} %get-tuple-element.29.refs_2_), channel_id=1, source_target_pairs={{0,2},{1,3},{2,0},{3,1},{4,6},{5,7},{6,4},{7,5},{8,10},{9,11},{10,... | collective-permute-start | bytes 1966088 | tf_op jit(solution)/shard_map/ppermute | solution.py:341
  202.1 32.2 %collective-permute-start.3 = (f32[4,8,40,128]{3,2,1,0:T(8,128)}, f32[4,8,40,128]{3,2,1,0:T(8,128)}, u32[]{:S(2)}, u32[]{:S(2)}) collective-permute-start(f32[4,8,40,128]{3,2,1,0:T(8,128)} %get-tuple-element.30.refs_3_), channel_id=1, source_target_pairs={{0,3},{1,0},{2,1},{3,2},{4,7},{5,4},{6,5},{7,6},{8,11},{9,8},{10,9... | collective-permute-start | bytes 1966088 | tf_op jit(solution)/shard_map/ppermute | solution.py:341
  216.6 17.7 %copy-start.3 = (f32[4,8,40,128]{3,2,1,0:T(8,128)S(1)}, f32[4,8,40,128]{3,2,1,0:T(8,128)}, u32[]{:S(2)}) copy-start(f32[4,8,40,128]{3,2,1,0:T(8,128)} %copy-done.2) | copy-start | bytes 1966084
  233.2 4.6 %copy-start.1 = (f32[4,8,4,2,16,128]{5,4,3,2,1,0:T(8,128)S(1)}, f32[4,8,4,2,16,128]{5,4,3,2,1,0:T(8,128)}, u32[]{:S(2)}) copy-start(f32[4,8,4,2,16,128]{5,4,3,2,1,0:T(8,128)} %get-tuple-element.36.refs_0_) | copy-start | bytes 6291460
  233.2 4.2 %collective-permute-start.10 = (f32[8,4,2,16,128]{4,3,2,1,0:T(8,128)}, f32[8,4,2,16,128]{4,3,2,1,0:T(8,128)}, u32[]{:S(2)}, u32[]{:S(2)}) collective-permute-start(f32[8,4,2,16,128]{4,3,2,1,0:T(8,128)} %get-tuple-element.40), channel_id=1, source_target_pairs={{0,4},{4,0},{1,5},{5,1},{2,6},{6,2},{3,7},{7,3},{8,12},{12,8},{9,1... | collective-permute-start | bytes 1572872 | tf_op jit(solution)/shard_map/ppermute | solution.py:294
  233.3 4.1 %collective-permute-start.7 = (f32[8,4,2,16,128]{4,3,2,1,0:T(8,128)}, f32[8,4,2,16,128]{4,3,2,1,0:T(8,128)}, u32[]{:S(2)}, u32[]{:S(2)}) collective-permute-start(f32[8,4,2,16,128]{4,3,2,1,0:T(8,128)} %get-tuple-element.37), channel_id=1, source_target_pairs={{0,4},{4,0},{1,5},{5,1},{2,6},{6,2},{3,7},{7,3},{8,12},{12,8},{9,1... | collective-permute-start | bytes 1572872 | tf_op jit(solution)/shard_map/ppermute | solution.py:294
  233.8 3.6 %collective-permute-start.8 = (f32[8,4,2,16,128]{4,3,2,1,0:T(8,128)}, f32[8,4,2,16,128]{4,3,2,1,0:T(8,128)}, u32[]{:S(2)}, u32[]{:S(2)}) collective-permute-start(f32[8,4,2,16,128]{4,3,2,1,0:T(8,128)} %get-tuple-element.38), channel_id=1, source_target_pairs={{0,4},{4,0},{1,5},{5,1},{2,6},{6,2},{3,7},{7,3},{8,12},{12,8},{9,1... | collective-permute-start | bytes 1572872 | tf_op jit(solution)/shard_map/ppermute | solution.py:294
  234.1 3.7 %collective-permute-start.9 = (f32[8,4,2,16,128]{4,3,2,1,0:T(8,128)}, f32[8,4,2,16,128]{4,3,2,1,0:T(8,128)}, u32[]{:S(2)}, u32[]{:S(2)}) collective-permute-start(f32[8,4,2,16,128]{4,3,2,1,0:T(8,128)} %get-tuple-element.39), channel_id=1, source_target_pairs={{0,4},{4,0},{1,5},{5,1},{2,6},{6,2},{3,7},{7,3},{8,12},{12,8},{9,1... | collective-permute-start | bytes 1572872 | tf_op jit(solution)/shard_map/ppermute | solution.py:294
  235.8 9.7 %collective-permute-start.4 = (f32[8,40,128]{2,1,0:T(8,128)S(1)}, f32[8,40,128]{2,1,0:T(8,128)S(1)}, u32[]{:S(2)}, u32[]{:S(2)}) collective-permute-start(f32[8,40,128]{2,1,0:T(8,128)S(1)} %get-tuple-element.32.refs_6_), channel_id=1, source_target_pairs={{0,8},{8,16},{16,24},{24,0},{1,9},{9,17},{17,25},{25,1},{2,10},{10... | collective-permute-start | bytes 491528 | tf_op jit(solution)/shard_map/ppermute | solution.py:341
  239.6 25.6 %collective-permute-start.11 = (f32[8,4,2,16,128]{4,3,2,1,0:T(8,128)S(1)}, f32[8,4,2,16,128]{4,3,2,1,0:T(8,128)S(1)}, u32[]{:S(2)}, u32[]{:S(2)}) collective-permute-start(f32[8,4,2,16,128]{4,3,2,1,0:T(8,128)S(1)} %get-tuple-element.42), channel_id=1, source_target_pairs={{0,1},{1,2},{2,3},{3,0},{4,5},{5,6},{6,7},{7,4},{8,9},{9,10},{10,1... | collective-permute-start | bytes 1572872 | tf_op jit(solution)/shard_map/ppermute | solution.py:341
  240.1 25.0 %collective-permute-start.12 = (f32[8,4,2,16,128]{4,3,2,1,0:T(8,128)S(1)}, f32[8,4,2,16,128]{4,3,2,1,0:T(8,128)S(1)}, u32[]{:S(2)}, u32[]{:S(2)}) collective-permute-start(f32[8,4,2,16,128]{4,3,2,1,0:T(8,128)S(1)} %get-tuple-element.43), channel_id=1, source_target_pairs={{0,2},{1,3},{2,0},{3,1},{4,6},{5,7},{6,4},{7,5},{8,10},{9,11},{10,... | collective-permute-start | bytes 1572872 | tf_op jit(solution)/shard_map/ppermute | solution.py:341
  242.5 24.0 %collective-permute-start.13 = (f32[8,4,2,16,128]{4,3,2,1,0:T(8,128)S(1)}, f32[8,4,2,16,128]{4,3,2,1,0:T(8,128)S(1)}, u32[]{:S(2)}, u32[]{:S(2)}) collective-permute-start(f32[8,4,2,16,128]{4,3,2,1,0:T(8,128)S(1)} %get-tuple-element.44), channel_id=1, source_target_pairs={{0,3},{1,0},{2,1},{3,2},{4,7},{5,4},{6,5},{7,6},{8,11},{9,8},{10,9... | collective-permute-start | bytes 1572872 | tf_op jit(solution)/shard_map/ppermute | solution.py:341
  242.5 7.2 %collective-permute-start.5 = (f32[8,40,128]{2,1,0:T(8,128)S(1)}, f32[8,40,128]{2,1,0:T(8,128)S(1)}, u32[]{:S(2)}, u32[]{:S(2)}) collective-permute-start(f32[8,40,128]{2,1,0:T(8,128)S(1)} %get-tuple-element.33.refs_7_), channel_id=1, source_target_pairs={{0,16},{8,24},{16,0},{24,8},{1,17},{9,25},{17,1},{25,9},{2,18},{10... | collective-permute-start | bytes 491528 | tf_op jit(solution)/shard_map/ppermute | solution.py:341
  245.5 7.7 %collective-permute-start.6 = (f32[8,40,128]{2,1,0:T(8,128)S(1)}, f32[8,40,128]{2,1,0:T(8,128)S(1)}, u32[]{:S(2)}, u32[]{:S(2)}) collective-permute-start(f32[8,40,128]{2,1,0:T(8,128)S(1)} %get-tuple-element.34.refs_8_), channel_id=1, source_target_pairs={{0,24},{8,0},{16,8},{24,16},{1,25},{9,1},{17,9},{25,17},{2,26},{10... | collective-permute-start | bytes 491528 | tf_op jit(solution)/shard_map/ppermute | solution.py:341

commit v5 on v4

--- a/solution.py
+++ b/solution.py
@@ -69,19 +69,19 @@
     return top, (value - top.astype(jnp.float32)).astype(jnp.bfloat16)
 
 
-def each_owner(pairs_ref, mine, store):
+def each_owner(pairs_ref, mine, store, first=0, count=NZ):
     def one(s, carry):
-        z, y = s // NY, s % NY
+        z, y = first + s // NY, s % NY
         k = ((z * NY + y) * NC + mine) * 2
         store(z, y, [(pairs_ref[2 * k + 2 * w], pairs_ref[2 * k + 2 * w + 1]) for w in range(2)])
         return carry
 
-    lax.fori_loop(0, NZ * NY, one, 0, unroll=4)
+    lax.fori_loop(0, count * NY, one, 0, unroll=4)
 
 
 def early_tiles(received, factors, pairs, core):
     width = received.shape[-1]
-    pieces = 4
+    pieces = 8
     held = PARTS // pieces
     total = NB * EA
     tall = 256
@@ -162,10 +162,15 @@
                     out[n, x, y, z, 0:EARLY] = jnp.where(lane[:EARLY] < EA, head, jnp.concatenate(gaps, axis=0))
                     out[n, x, y, z, EARLY:PACKED] = tail[:EARLY - 8]
 
-            each_owner(pairs_ref, who, store)
-            send = pltpu.make_async_copy(out.at[n], dst, sems.at[pieces + 1 + n])
-            send.start()
-            sends.append(send)
+            for h in range(2):
+                zs = pl.ds(h * NZ // 2, NZ // 2)
+                each_owner(pairs_ref, who, store, h * NZ // 2, NZ // 2)
+                sends.append(
+                    pltpu.make_async_copy(
+                        out.at[n, :, :, zs], dst.at[:, :, zs], sems.at[pieces + 1 + 2 * n + h]
+                    )
+                )
+                sends[-1].start()
         for send in sends:
             send.wait()
         save.wait()
@@ -183,7 +188,7 @@
                 pltpu.VMEM((2, total, width), jnp.bfloat16),
                 pltpu.VMEM((total, NB * BS), jnp.float32),
                 pltpu.VMEM((2,) + shape, jnp.float32),
-                pltpu.SemaphoreType.DMA((pieces + 3,)),
+                pltpu.SemaphoreType.DMA((pieces + 5,)),
             ],
         ),
         out_shape=[jax.ShapeDtypeStruct(shape, jnp.float32)] * 2
@@ -221,19 +226,20 @@
         lax.fori_loop(0, NB, convert, 0)
 
         def column(g, carry):
-            for h in range(NB // 2):
+            for h in range(NB // 4):
 
                 @pl.when(g == h)
                 def _(h=h):
-                    loads[h].wait()
-
-            bh, bl = (halves[part, pl.ds(2 * g, 2)].reshape(2 * BS, width) for part in (0, 1))
+                    loads[2 * h].wait()
+                    loads[2 * h + 1].wait()
+
+            bh, bl = (halves[part, pl.ds(4 * g, 4)].reshape(4 * BS, width) for part in (0, 1))
             ah, al = late[0], late[1]
-            cols = pl.ds(pl.multiple_of(g * 256, 256), 256)
+            cols = pl.ds(pl.multiple_of(g * 512, 512), 512)
             prod[:, cols] = dot(ah, bh) + (dot(ah, bl) + dot(al, bh))
             return carry
 
-        lax.fori_loop(0, NB // 2, column, 0)
+        lax.fori_loop(0, NB // 4, column, 0)
         lane = lax.broadcasted_iota(jnp.int32, (LATE, BS), 1)
         masks = {far: (lane // (far * EARLY)) % 2 == 0 for far in (2, 1)}
 
@@ -421,7 +427,7 @@
     give, keep, kept = early_tiles(early, factors, listed, core)
     kept = kept.reshape(2, NB, EA, -1)
     parts = total("x", [keep, swap_cores(give)], [])
-    keep, *gives = late_tiles(late, kept, factors, listed, core, *parts)
+    keep, *gives = late_tiles(late, kept, factors, listed, core, *parts[1:])
     parts = total("y", send_on("x", parts), [])
     rest = total("x", [keep], [swap_cores(give) for give in gives], *parts)
     parts = merge(send_on("y", parts))

time: 293 us -> 292 us (level)
  transfers between devices with their start and end apart: 16 -> 16, of which waited for: 7 -> 7; matrix products, arithmetic and copies ran while one was open for 1% -> 1% of each run, Pallas kernels for 17% -> 16%
where the time goes in v5:
time: 292 us; the launch traced here: 291 us
  waiting for transfers between devices  166 us (57%)
  Pallas kernels  54.5 us (19%)
  blocking collectives  36.3 us (12%)
  starting transfers between devices  31 us (11%)
    all_to_all x1, waiting for transfers between devices, on_device(): early = lax.all_to_all(relayout(jac, 0, EARLY), OBS_AXES, 0, 0, tiled=True)  136 us
    all_to_all x1, blocking collectives, on_device(): rest = lax.all_to_all(rest, ('z', 'y'), 0, 0, tiled=True)  24.5 us
    pallas_call x1, Pallas kernels, early_tiles(): pl.pallas_call(body, grid_spec=pltpu.PrefetchScalarGridSpec(num_scalar_pr...  23.5 us
    all_to_all x1, waiting for transfers between devices, on_device(): lax.all_to_all(relayout(jac, EARLY, LATE), OBS_AXES, 0, 0, tiled=True)  16 us
    pallas_call x1, Pallas kernels, late_tiles(): pl.pallas_call(body, grid_spec=pltpu.PrefetchScalarGridSpec(num_scalar_pr...  15.8 us
    all_to_all x1, starting transfers between devices, on_device(): early = lax.all_to_all(relayout(jac, 0, EARLY), OBS_AXES, 0, 0, tiled=True)  12.3 us
    all_to_all x1, blocking collectives, on_device(): parts = lax.all_to_all(parts, 'z', 0, 0, tiled=True)  11.8 us
    ppermute x9, starting transfers between devices, send_on(): lax.ppermute(parts[d], axis, [(s, (s + d) % size) for s in range(size)])  11.6 us
  transfers between devices with their start and end apart: 16, of which 7 were waited for; matrix products, arithmetic and copies ran while one was open for 1% of the time, Pallas kernels for 16%

profile of v5, /device:TPU:6, one launch (start us, length us, event | category | flops | bytes accessed | tf_op | source)
XLA Modules:
  0.0 291.2 jit_solution(16622458644225081622)
XLA Ops:
  0.0 6.0 %relayout.2 = f32[64,24,1024]{2,1,0:T(8,128)} custom-call(f32[32,65536]{1,0:T(8,128)} %src.3), custom_call_target="tpu_custom_call" | custom-call | flops 1 | bytes 1 | tf_op jit(solution)/shard_map/relayout/pallas_call | solution.py:48
  6.0 12.3 %all-to-all-start = ((f32[64,24,1024]{2,1,0:T(8,128)}), f32[64,24,1024]{2,1,0:T(8,128)}, u32[]{:S(2)}, u32[]{:S(2)}) async-start(f32[64,24,1024]{2,1,0:T(8,128)} %relayout.2), calls=%async_computation | async-start | bytes 12582912 | tf_op jit(solution)/shard_map/all_to_all | solution.py:424
  18.4 3.0 %relayout.3 = f32[64,8,1024]{2,1,0:T(8,128)} custom-call(f32[32,65536]{1,0:T(8,128)} %src.3), custom_call_target="tpu_custom_call" | custom-call | flops 1 | bytes 1 | tf_op jit(solution)/shard_map/relayout/pallas_call | solution.py:48
  23.1 136.5 %all-to-all-done.src = f32[64,24,1024]{2,1,0:T(8,128)} async-done(((f32[64,24,1024]{2,1,0:T(8,128)}), f32[64,24,1024]{2,1,0:T(8,128)}, u32[]{:S(2)}, u32[]{:S(2)}) %all-to-all-start) | async-done | bytes 6291488 | tf_op jit(solution)/shard_map/all_to_all | solution.py:424
  159.6 5.9 %all-to-all-start.2 = ((f32[64,8,1024]{2,1,0:T(8,128)}), f32[64,8,1024]{2,1,0:T(8,128)}, u32[]{:S(2)}, u32[]{:S(2)}) async-start(f32[64,8,1024]{2,1,0:T(8,128)} %relayout.3), calls=%async_computation.2 | async-start | bytes 4194304 | tf_op jit(solution)/shard_map/all_to_all | solution.py:425
  165.4 23.5 %early_tiles.1 = (f32[4,4,8,40,128]{4,3,2,1,0:T(8,128)}, f32[4,4,8,40,128]{4,3,2,1,0:T(8,128)}, bf16[2,1536,1024]{2,1,0:T(8,128)(2,1)}) custom-call(s32[256]{0:T(256)} %reshape.29.pairs_ref, s32[1]{0:T(128)} %bitcast.2.core_ref, f32[16,1024]{1,0:T(8,128)} %broadcast_multiply_fusion.fac, f32[64,24,1024]{2,1,0:T(8,128)} %all-to-all-done.src), custom_call_target="tpu_custom_call" | custom-call | flops 99999997952 | bytes 18874368 | tf_op jit(solution)/shard_map/early_tiles/pallas_call | solution.py:179
  189.0 5.1 %collective-permute-done.refs_1_ = f32[4,4,8,40,128]{4,3,2,1,0:T(8,128)S(1)} collective-permute-done((f32[4,4,8,40,128]{4,3,2,1,0:T(8,128)}, f32[4,4,8,40,128]{4,3,2,1,0:T(8,128)S(1)}, u32[]{:S(2)}, u32[]{:S(2)}) %collective-permute-start) | collective-permute-done | bytes 2621472 | tf_op jit(solution)/shard_map/ppermute | solution.py:300
  194.2 1.7 copy-done
  195.9 1.9 total.3
  198.2 2.5 collective-permute-start.2
  200.7 16.0 %all-to-all-done.2.src = f32[64,8,1024]{2,1,0:T(8,128)} async-done(((f32[64,8,1024]{2,1,0:T(8,128)}), f32[64,8,1024]{2,1,0:T(8,128)}, u32[]{:S(2)}, u32[]{:S(2)}) %all-to-all-start.2) | async-done | bytes 2097184 | tf_op jit(solution)/shard_map/all_to_all | solution.py:425
  216.6 15.8 %late_tiles.1 = (f32[4,8,4,2,16,128]{5,4,3,2,1,0:T(8,128)}, f32[8,4,2,16,128]{4,3,2,1,0:T(8,128)}, f32[8,4,2,16,128]{4,3,2,1,0:T(8,128)}, f32[8,4,2,16,128]{4,3,2,1,0:T(8,128)}, f32[8,4,2,16,128]{4,3,2,1,0:T(8,128)}) custom-call(s32[256]{0:T(256)} %reshape.29.pairs_ref, s32[1]{0:T(128)} %bitcast.2.core_ref, f32[64,8,1024]{2,1,0:T(8,128)} %all-to-all-done.2.src, ...), custom_call_target="tpu_custom_call" | custom-call | flops 99999997952 | bytes 12582912 | tf_op jit(solution)/shard_map/late_tiles/pallas_call | solution.py:276
  233.5 1.7 total.4
  235.2 1.5 collective-permute-start.4
  237.0 1.6 total.5
  239.2 2.4 collective-permute-start.12
  241.6 3.0 %collective-permute-start.5 = (f32[8,40,128]{2,1,0:T(8,128)S(1)}, f32[8,40,128]{2,1,0:T(8,128)S(1)}, u32[]{:S(2)}, u32[]{:S(2)}) collective-permute-start(f32[8,40,128]{2,1,0:T(8,128)S(1)} %get-tuple-element.33.refs_7_), channel_id=1, source_target_pairs={{0,16},{8,24},{16,0},{24,8},{1,17},{9,25},{17,1},{25,9},{2,18},{10... | collective-permute-start | bytes 491528 | tf_op jit(solution)/shard_map/ppermute | solution.py:347
  244.6 1.2 collective-permute-start.6
  245.8 3.0 %collective-permute-done.5.refs_2_ = f32[8,40,128]{2,1,0:T(8,128)S(1)} collective-permute-done((f32[8,40,128]{2,1,0:T(8,128)S(1)}, f32[8,40,128]{2,1,0:T(8,128)S(1)}, u32[]{:S(2)}, u32[]{:S(2)}) %collective-permute-start.5) | collective-permute-done | bytes 163872 | tf_op jit(solution)/shard_map/ppermute | solution.py:347
  248.8 3.6 %collective-permute-done.6.refs_3_ = f32[8,40,128]{2,1,0:T(8,128)S(1)} collective-permute-done((f32[8,40,128]{2,1,0:T(8,128)S(1)}, f32[8,40,128]{2,1,0:T(8,128)S(1)}, u32[]{:S(2)}, u32[]{:S(2)}) %collective-permute-start.6) | collective-permute-done | bytes 163872 | tf_op jit(solution)/shard_map/ppermute | solution.py:347
  252.4 11.8 %all_to_all.20.refs_4_.first = f32[8,40,128]{2,1,0:T(8,128)S(1)} all-to-all(f32[8,40,128]{2,1,0:T(8,128)S(1)} %merge.2), channel_id=1, replica_groups=mesh['z'=8,'y'=4,'c'=2,'x'=4] {'z'}, dimensions={0} | all-to-all | bytes 327680 | tf_op jit(solution)/shard_map/all_to_all | solution.py:434
  264.3 1.4 collective-permute-done.13.refs_3_
  265.8 24.5 %all_to_all.21.second = f32[32,2,16,128]{3,2,1,0:T(8,128)S(1)} all-to-all(f32[32,2,16,128]{3,2,1,0:T(8,128)S(1)} %bitcast.8), channel_id=1, replica_groups=mesh['z'=8,'y'=4,'c'=2,'x'=4] {'z','y'}, dimensions={0} | all-to-all | bytes 1048576 | tf_op jit(solution)/shard_map/all_to_all | solution.py:436
  290.3 0.9 finish.1
  (37 shorter events, 4.2 us)
Async XLA Ops:
  6.0 153.5 %all-to-all-start = ((f32[64,24,1024]{2,1,0:T(8,128)}), f32[64,24,1024]{2,1,0:T(8,128)}, u32[]{:S(2)}, u32[]{:S(2)}) async-start(f32[64,24,1024]{2,1,0:T(8,128)} %relayout.2), calls=%async_computation | async-start | bytes 12582912 | tf_op jit(solution)/shard_map/all_to_all | solution.py:424
  18.4 3.1 %copy-start.3 = (s32[128,2]{0,1:T(2,128)S(1)}, s32[128,2]{0,1:T(2,128)}, u32[]{:S(2)}) copy-start(s32[128,2]{0,1:T(2,128)} %param.9) | copy-start | bytes 3076
  18.4 3.9 %copy-start.2 = (s32[1,1024]{1,0:T(1,128)S(1)}, s32[1,1024]{1,0:T(1,128)}, u32[]{:S(2)}) copy-start(s32[1,1024]{1,0:T(1,128)} %param.6) | copy-start | bytes 12292
  18.4 3.9 %copy-start.4 = (f32[16]{0:T(128)S(1)}, f32[16]{0:T(128)}, u32[]{:S(2)}) copy-start(f32[16]{0:T(128)} %param.7) | copy-start | bytes 196
  18.4 3.9 %copy-start.5 = (s32[1,1,16]{2,1,0:T(1,128)S(1)}, s32[1,1,16]{2,1,0:T(1,128)}, u32[]{:S(2)}) copy-start(s32[1,1,16]{2,1,0:T(1,128)} %param.8) | copy-start | bytes 196
  159.6 57.1 %all-to-all-start.2 = ((f32[64,8,1024]{2,1,0:T(8,128)}), f32[64,8,1024]{2,1,0:T(8,128)}, u32[]{:S(2)}, u32[]{:S(2)}) async-start(f32[64,8,1024]{2,1,0:T(8,128)} %relayout.3), calls=%async_computation.2 | async-start | bytes 4194304 | tf_op jit(solution)/shard_map/all_to_all | solution.py:425
  188.9 5.2 %collective-permute-start = (f32[4,4,8,40,128]{4,3,2,1,0:T(8,128)}, f32[4,4,8,40,128]{4,3,2,1,0:T(8,128)S(1)}, u32[]{:S(2)}, u32[]{:S(2)}) collective-permute-start(f32[4,4,8,40,128]{4,3,2,1,0:T(8,128)} %get-tuple-element.26), channel_id=1, source_target_pairs={{0,4},{4,0},{1,5},{5,1},{2,6},{6,2},{3,7},{7,3},{8,12},{12,8},{9,1... | collective-permute-start | bytes 7864328 | tf_op jit(solution)/shard_map/ppermute | solution.py:300
  194.1 1.7 copy-start
  197.8 35.3 %collective-permute-start.1 = (f32[4,8,40,128]{3,2,1,0:T(8,128)}, f32[4,8,40,128]{3,2,1,0:T(8,128)}, u32[]{:S(2)}, u32[]{:S(2)}) collective-permute-start(f32[4,8,40,128]{3,2,1,0:T(8,128)} %get-tuple-element.28.refs_0_), channel_id=1, source_target_pairs={{0,1},{1,2},{2,3},{3,0},{4,5},{5,6},{6,7},{7,4},{8,9},{9,10},{10,1... | collective-permute-start | bytes 1966088 | tf_op jit(solution)/shard_map/ppermute | solution.py:347
  198.2 34.9 %collective-permute-start.2 = (f32[4,8,40,128]{3,2,1,0:T(8,128)}, f32[4,8,40,128]{3,2,1,0:T(8,128)}, u32[]{:S(2)}, u32[]{:S(2)}) collective-permute-start(f32[4,8,40,128]{3,2,1,0:T(8,128)} %get-tuple-element.29.refs_1_), channel_id=1, source_target_pairs={{0,2},{1,3},{2,0},{3,1},{4,6},{5,7},{6,4},{7,5},{8,10},{9,11},{10,... | collective-permute-start | bytes 1966088 | tf_op jit(solution)/shard_map/ppermute | solution.py:347
  200.7 32.9 %collective-permute-start.3 = (f32[4,8,40,128]{3,2,1,0:T(8,128)}, f32[4,8,40,128]{3,2,1,0:T(8,128)}, u32[]{:S(2)}, u32[]{:S(2)}) collective-permute-start(f32[4,8,40,128]{3,2,1,0:T(8,128)} %get-tuple-element.30.refs_2_), channel_id=1, source_target_pairs={{0,3},{1,0},{2,1},{3,2},{4,7},{5,4},{6,5},{7,6},{8,11},{9,8},{10,9... | collective-permute-start | bytes 1966088 | tf_op jit(solution)/shard_map/ppermute | solution.py:347
  232.4 4.6 %copy-start.1 = (f32[4,8,4,2,16,128]{5,4,3,2,1,0:T(8,128)S(1)}, f32[4,8,4,2,16,128]{5,4,3,2,1,0:T(8,128)}, u32[]{:S(2)}) copy-start(f32[4,8,4,2,16,128]{5,4,3,2,1,0:T(8,128)} %get-tuple-element.36.refs_0_) | copy-start | bytes 6291460
  232.4 4.4 %collective-permute-start.10 = (f32[8,4,2,16,128]{4,3,2,1,0:T(8,128)}, f32[8,4,2,16,128]{4,3,2,1,0:T(8,128)S(1)}, u32[]{:S(2)}, u32[]{:S(2)}) collective-permute-start(f32[8,4,2,16,128]{4,3,2,1,0:T(8,128)} %get-tuple-element.40), channel_id=1, source_target_pairs={{0,4},{4,0},{1,5},{5,1},{2,6},{6,2},{3,7},{7,3},{8,12},{12,8},{9,1... | collective-permute-start | bytes 1572872 | tf_op jit(solution)/shard_map/ppermute | solution.py:300
  232.5 4.3 %collective-permute-start.7 = (f32[8,4,2,16,128]{4,3,2,1,0:T(8,128)}, f32[8,4,2,16,128]{4,3,2,1,0:T(8,128)}, u32[]{:S(2)}, u32[]{:S(2)}) collective-permute-start(f32[8,4,2,16,128]{4,3,2,1,0:T(8,128)} %get-tuple-element.37), channel_id=1, source_target_pairs={{0,4},{4,0},{1,5},{5,1},{2,6},{6,2},{3,7},{7,3},{8,12},{12,8},{9,1... | collective-permute-start | bytes 1572872 | tf_op jit(solution)/shard_map/ppermute | solution.py:300
  233.0 3.8 %collective-permute-start.8 = (f32[8,4,2,16,128]{4,3,2,1,0:T(8,128)}, f32[8,4,2,16,128]{4,3,2,1,0:T(8,128)}, u32[]{:S(2)}, u32[]{:S(2)}) collective-permute-start(f32[8,4,2,16,128]{4,3,2,1,0:T(8,128)} %get-tuple-element.38), channel_id=1, source_target_pairs={{0,4},{4,0},{1,5},{5,1},{2,6},{6,2},{3,7},{7,3},{8,12},{12,8},{9,1... | collective-permute-start | bytes 1572872 | tf_op jit(solution)/shard_map/ppermute | solution.py:300
  233.1 3.9 %collective-permute-start.9 = (f32[8,4,2,16,128]{4,3,2,1,0:T(8,128)}, f32[8,4,2,16,128]{4,3,2,1,0:T(8,128)}, u32[]{:S(2)}, u32[]{:S(2)}) collective-permute-start(f32[8,4,2,16,128]{4,3,2,1,0:T(8,128)} %get-tuple-element.39), channel_id=1, source_target_pairs={{0,4},{4,0},{1,5},{5,1},{2,6},{6,2},{3,7},{7,3},{8,12},{12,8},{9,1... | collective-permute-start | bytes 1572872 | tf_op jit(solution)/shard_map/ppermute | solution.py:300
  235.2 9.4 %collective-permute-start.4 = (f32[8,40,128]{2,1,0:T(8,128)S(1)}, f32[8,40,128]{2,1,0:T(8,128)S(1)}, u32[]{:S(2)}, u32[]{:S(2)}) collective-permute-start(f32[8,40,128]{2,1,0:T(8,128)S(1)} %get-tuple-element.32.refs_6_), channel_id=1, source_target_pairs={{0,8},{8,16},{16,24},{24,0},{1,9},{9,17},{17,25},{25,1},{2,10},{10... | collective-permute-start | bytes 491528 | tf_op jit(solution)/shard_map/ppermute | solution.py:347
  238.7 25.6 %collective-permute-start.11 = (f32[8,4,2,16,128]{4,3,2,1,0:T(8,128)S(1)}, f32[8,4,2,16,128]{4,3,2,1,0:T(8,128)S(1)}, u32[]{:S(2)}, u32[]{:S(2)}) collective-permute-start(f32[8,4,2,16,128]{4,3,2,1,0:T(8,128)S(1)} %get-tuple-element.42), channel_id=1, source_target_pairs={{0,1},{1,2},{2,3},{3,0},{4,5},{5,6},{6,7},{7,4},{8,9},{9,10},{10,1... | collective-permute-start | bytes 1572872 | tf_op jit(solution)/shard_map/ppermute | solution.py:347
  239.2 25.0 %collective-permute-start.12 = (f32[8,4,2,16,128]{4,3,2,1,0:T(8,128)S(1)}, f32[8,4,2,16,128]{4,3,2,1,0:T(8,128)S(1)}, u32[]{:S(2)}, u32[]{:S(2)}) collective-permute-start(f32[8,4,2,16,128]{4,3,2,1,0:T(8,128)S(1)} %get-tuple-element.43), channel_id=1, source_target_pairs={{0,2},{1,3},{2,0},{3,1},{4,6},{5,7},{6,4},{7,5},{8,10},{9,11},{10,... | collective-permute-start | bytes 1572872 | tf_op jit(solution)/shard_map/ppermute | solution.py:347
  241.6 24.0 %collective-permute-start.13 = (f32[8,4,2,16,128]{4,3,2,1,0:T(8,128)S(1)}, f32[8,4,2,16,128]{4,3,2,1,0:T(8,128)S(1)}, u32[]{:S(2)}, u32[]{:S(2)}) collective-permute-start(f32[8,4,2,16,128]{4,3,2,1,0:T(8,128)S(1)} %get-tuple-element.44), channel_id=1, source_target_pairs={{0,3},{1,0},{2,1},{3,2},{4,7},{5,4},{6,5},{7,6},{8,11},{9,8},{10,9... | collective-permute-start | bytes 1572872 | tf_op jit(solution)/shard_map/ppermute | solution.py:347
  241.6 7.2 %collective-permute-start.5 = (f32[8,40,128]{2,1,0:T(8,128)S(1)}, f32[8,40,128]{2,1,0:T(8,128)S(1)}, u32[]{:S(2)}, u32[]{:S(2)}) collective-permute-start(f32[8,40,128]{2,1,0:T(8,128)S(1)} %get-tuple-element.33.refs_7_), channel_id=1, source_target_pairs={{0,16},{8,24},{16,0},{24,8},{1,17},{9,25},{17,1},{25,9},{2,18},{10... | collective-permute-start | bytes 491528 | tf_op jit(solution)/shard_map/ppermute | solution.py:347
  244.6 7.7 %collective-permute-start.6 = (f32[8,40,128]{2,1,0:T(8,128)S(1)}, f32[8,40,128]{2,1,0:T(8,128)S(1)}, u32[]{:S(2)}, u32[]{:S(2)}) collective-permute-start(f32[8,40,128]{2,1,0:T(8,128)S(1)} %get-tuple-element.34.refs_8_), channel_id=1, source_target_pairs={{0,24},{8,0},{16,8},{24,16},{1,25},{9,1},{17,9},{25,17},{2,26},{10... | collective-permute-start | bytes 491528 | tf_op jit(solution)/shard_map/ppermute | solution.py:347
